TPU v7x, 128 devices: a whole 4x4x4 slice. The times are simulated.
128 devices in a mesh: row: 16 (over x, z), col: 4 (over y_lo, core), grp: 2 (over y_hi).
Axes of the slice: x: 4, y: 4 (y_hi: 2, y_lo: 2; y = y_hi * 2 + y_lo), z: 4, core: 2. Of those that a mesh axis runs over, the one named last changes fastest.
Arguments:
- matrix: float32 [16384, 16384], P('row', ('col', 'grp')), may hold values from -8 to 8, as said below
- basis_rows: float32 [4096, 16384], P(('col', 'grp'), 'row'), may hold values from -6 to 6
- reflectors: float32 [16384, 512], P('row'), may hold values from -0.125 to 0.125
- tfactor: float32 [512, 512], replicated, may hold values from -0.25 to 2, as said below
Outputs:
- new_matrix: float32 [16384, 16384], P('row', ('col', 'grp'))
- new_basis: float32 [4096, 16384], P(('col', 'grp'), 'row')
Inputs may be any that keep to these rules, and one draw needn't show every extreme that they name: The matrix A that it represents is symmetric. `tfactor`: upper triangular: zero below the diagonal, diagonal between 1 and 2.
All inputs are finite; a program needn't handle non-finite values.
Results may differ from a plain program's by a relative error of at most 0.000073.
Values sent between devices are 32-bit elements; how exact they have to be, the bound alone decides.
No kernel may reach another device: no remote copies, remote signals or barrier semaphores. Data moves between devices by JAX's collectives and lax.ppermute only.
A program may use at most 128 MiB of HBM per device.

v0:
```python
import functools

import jax
import jax.numpy as jnp
import numpy as np
from jax import lax
from jax.experimental import pallas as pl
from jax.experimental.pallas import tpu as pltpu
from jax.sharding import PartitionSpec as P

F32, BF16 = jnp.float32, jnp.bfloat16
EVERY = ("row", "col", "grp")
NN = (((1,), (0,)), ((), ()))
NT = (((1,), (1,)), ((), ()))
TN = (((0,), (0,)), ((), ()))


def flip_ring(i, bit):
    g = (i ^ (i >> 1)) ^ (1 << bit)
    return g ^ (g >> 1)


def linear(x, z, y, core):
    return (x * 4 + z) * 8 + ((y % 2) * 2 + core) * 2 + y // 2


def coords(dev):
    row, member = divmod(dev, 8)
    return row // 4, row % 4, (member % 2) * 2 + member // 4, (member // 2) % 2


def flip(dev, dim):
    x, z, y, core = coords(dev)
    if dim == "c":
        return linear(x, z, y, 1 - core)
    bit = int(dim[1])
    if dim[0] == "x":
        x = flip_ring(x, bit)
    elif dim[0] == "z":
        z = flip_ring(z, bit)
    else:
        y = flip_ring(y, bit)
    return linear(x, z, y, core)


ROW_DIMS = ("x0", "z0", "x1", "z1")


def row_dim(core, half, step):
    return ROW_DIMS[(step + core * 2 + half) % 4]


def y_dim(core, step):
    return "y%d" % ((step + core) % 2)


def relative(dev, dims, j):
    for k, dim in enumerate(dims):
        if j >> k & 1:
            dev = flip(dev, dim)
    return dev


def build_tables():
    out = np.zeros((128, 64), np.int32)
    for dev in range(128):
        core = coords(dev)[3]
        for h in range(2):
            dims = [row_dim(core, h, s) for s in range(4)]
            for j in range(16):
                out[dev, h * 16 + j] = relative(dev, dims, j) // 8
        other = flip(dev, "c")
        for first, base in ((other, 32), (dev, 36)):
            dims = [y_dim(coords(first)[3], s) for s in range(2)]
            for j in range(4):
                out[dev, base + j] = relative(first, dims, j) % 8
        out[dev, 40] = dev % 8
    return out


TABLES = build_tables()


def moved(x, dim_of_core):
    pairs = [(dev, flip(dev, dim_of_core(coords(dev)[3]))) for dev in range(128)]
    return lax.ppermute(x, EVERY, pairs)


def split(x):
    hi = x.astype(BF16)
    return hi, (x - hi.astype(F32)).astype(BF16)


def dot3(a, b, dims):
    def one(u, v):
        return lax.dot_general(u, v, dims, preferred_element_type=F32)

    return one(a[0], b[0]) + (one(a[0], b[1]) + one(a[1], b[0]))


def cost(macs, moved_bytes):
    return pl.CostEstimate(flops=6 * macs, bytes_accessed=moved_bytes, transcendentals=0)


def params(mib):
    return pltpu.CompilerParams(vmem_limit_bytes=mib * 2**20)


def full(shape):
    return pl.BlockSpec(shape, lambda *_: (0,) * len(shape))


def basis_kernel(tab, b_ref, v_ref, q0_ref, q1_ref, q):
    q[...] = dot3(split(b_ref[...]), split(v_ref[...]), NN)
    for h, out in enumerate((q0_ref, q1_ref)):
        for j in range(16):
            place = int("{:04b}".format(j)[::-1], 2)
            rows = pl.ds(pl.multiple_of(tab[h * 16 + j] * 32, 32), 32)
            out[place * 32 : place * 32 + 32, :] = q[rows, h * 256 : h * 256 + 256]


def basis_product(tab, basis, v):
    return pl.pallas_call(
        basis_kernel,
        grid_spec=pltpu.PrefetchScalarGridSpec(
            num_scalar_prefetch=1,
            grid=(1,),
            in_specs=[full((512, 1024)), full((1024, 512))],
            out_specs=[full((512, 256))] * 2,
            scratch_shapes=[pltpu.VMEM((512, 512), F32)],
        ),
        out_shape=[jax.ShapeDtypeStruct((512, 256), F32)] * 2,
        compiler_params=params(32),
        cost_estimate=cost(512 * 1024 * 512, 5 << 20),
    )(tab, basis, v)


def place_blocks(tab, pieces, hi, lo, rows=128):
    for h in range(2):
        for j in range(16):
            src = pieces[h * 2 + j // 8]
            block = src[(j % 8) * rows : (j % 8) * rows + rows, :]
            bh, bl = split(block)
            at = pl.ds(pl.multiple_of(tab[h * 16 + j] * rows, rows), rows)
            hi[at, h * 256 : h * 256 + 256] = bh
            lo[at, h * 256 : h * 256 + 256] = bl


def apply_kernel(tab, a0, a1, a2, a3, p0, p1, p2, p3, send_ref, keep_ref, vh, vl):
    step = pl.program_id(0)

    @pl.when(step == 0)
    def _():
        place_blocks(tab, (p0, p1, p2, p3), vh, vl)

    def product(out):
        for i, a in enumerate((a0, a1, a2, a3)):
            out[i * 128 : i * 128 + 128, :] = dot3(
                split(a[...]), (vh[...], vl[...]), NN
            )

    @pl.when(step == 0)
    def _():
        product(send_ref)

    @pl.when(step == 1)
    def _():
        product(keep_ref)


def apply_matrix(tab, matrix, pieces):
    def a_spec(i):
        return pl.BlockSpec((128, 2048), lambda s, t, i=i: (t[32 + s * 4 + i], 0))

    return pl.pallas_call(
        apply_kernel,
        grid_spec=pltpu.PrefetchScalarGridSpec(
            num_scalar_prefetch=1,
            grid=(2,),
            in_specs=[a_spec(i) for i in range(4)] + [full((1024, 256))] * 4,
            out_specs=[full((512, 512))] * 2,
            scratch_shapes=[pltpu.VMEM((2048, 512), BF16)] * 2,
        ),
        out_shape=[jax.ShapeDtypeStruct((512, 512), F32)] * 2,
        compiler_params=params(40),
        cost_estimate=cost(1024 * 2048 * 512, 14 << 20),
    )(tab, matrix, matrix, matrix, matrix, *pieces)


def inner_kernel(tab, v_ref, s_ref, k_ref, gs_ref, gk_ref, g):
    total = None
    for base, src in ((32, s_ref), (36, k_ref)):
        rows = [
            v_ref[pl.ds(pl.multiple_of(tab[base + i] * 128, 128), 128), :]
            for i in range(4)
        ]
        v = jnp.concatenate(rows, axis=0)
        part = dot3(split(v), split(src[...]), TN)
        total = part if total is None else total + part
    g[...] = total
    for base, out in ((32, gs_ref), (36, gk_ref)):
        for i in range(4):
            at = pl.ds(pl.multiple_of(tab[base + i] * 64, 64), 64)
            out[i * 64 : i * 64 + 64, :] = g[at, :]


def inner_product(tab, v, send, keep):
    return pl.pallas_call(
        inner_kernel,
        grid_spec=pltpu.PrefetchScalarGridSpec(
            num_scalar_prefetch=1,
            grid=(1,),
            in_specs=[full((1024, 512)), full((512, 512)), full((512, 512))],
            out_specs=[full((256, 512))] * 2,
            scratch_shapes=[pltpu.VMEM((512, 512), F32)],
        ),
        out_shape=[jax.ShapeDtypeStruct((256, 512), F32)] * 2,
        compiler_params=params(32),
        cost_estimate=cost(1024 * 512 * 512, 5 << 20),
    )(tab, v, send, keep)


def turned_kernel(tab, t_ref, v_ref, p0, p1, p2, p3, ch, cl, rh, rl, vh, vl):
    t = split(t_ref[...])
    place_blocks(tab, (p0, p1, p2, p3), vh, vl)
    for i in range(4):
        at = slice(i * 512, i * 512 + 512)
        ch[at, :], cl[at, :] = split(dot3((vh[at, :], vl[at, :]), t, NT))
    for i in range(2):
        at = slice(i * 512, i * 512 + 512)
        rh[at, :], rl[at, :] = split(dot3(split(v_ref[at, :]), t, NT))


def turned(tab, tfactor, v, pieces):
    return pl.pallas_call(
        turned_kernel,
        grid_spec=pltpu.PrefetchScalarGridSpec(
            num_scalar_prefetch=1,
            grid=(1,),
            in_specs=[full((512, 512)), full((1024, 512))] + [full((1024, 256))] * 4,
            out_specs=[full((2048, 512))] * 2 + [full((1024, 512))] * 2,
            scratch_shapes=[pltpu.VMEM((2048, 512), BF16)] * 2,
        ),
        out_shape=[jax.ShapeDtypeStruct((2048, 512), BF16)] * 2
        + [jax.ShapeDtypeStruct((1024, 512), BF16)] * 2,
        compiler_params=params(48),
        cost_estimate=cost(3072 * 512 * 512, 13 << 20),
    )(tab, tfactor, v, *pieces)


def rows_kernel(tab, wk_ref, ws_ref, gk_ref, gs_ref, rh, rl, oh, ol, g, w):
    for base, gsrc, wsrc in ((36, gk_ref, wk_ref), (32, gs_ref, ws_ref)):
        for i in range(4):
            g[pl.ds(pl.multiple_of(tab[base + i] * 64, 64), 64), :] = gsrc[
                i * 64 : i * 64 + 64, :
            ]
            w[pl.ds(pl.multiple_of(tab[base + i] * 128, 128), 128), :] = wsrc[
                i * 128 : i * 128 + 128, :
            ]
    gg = split(g[...])
    for i in range(2):
        at = slice(i * 512, i * 512 + 512)
        oh[at, :], ol[at, :] = split(w[at, :] - dot3((rh[at, :], rl[at, :]), gg, NN))


def rows_less(tab, w_keep, w_other, g_keep, g_other, rh, rl):
    return pl.pallas_call(
        rows_kernel,
        grid_spec=pltpu.PrefetchScalarGridSpec(
            num_scalar_prefetch=1,
            grid=(1,),
            in_specs=[full((512, 512))] * 2
            + [full((256, 512))] * 2
            + [full((1024, 512))] * 2,
            out_specs=[full((1024, 512))] * 2,
            scratch_shapes=[pltpu.VMEM((512, 512), F32), pltpu.VMEM((1024, 512), F32)],
        ),
        out_shape=[jax.ShapeDtypeStruct((1024, 512), BF16)] * 2,
        compiler_params=params(40),
        cost_estimate=cost(1024 * 512 * 512, 7 << 20),
    )(tab, w_keep, w_other, g_keep, g_other, rh, rl)


def update_kernel(tab, a, p0, p1, p2, p3, ch, cl, rh, rl, oh, ol, out, wh, wl, lh, ll):
    step = pl.program_id(0)

    @pl.when(step == 0)
    def _():
        place_blocks(tab, (p0, p1, p2, p3), wh, wl)
        lh[:, :512] = rh[...]
        ll[:, :512] = rl[...]
        lh[:, 512:] = oh[...]
        ll[:, 512:] = ol[...]

    at = pl.ds(pl.multiple_of(step * 256, 256), 256)
    right_h = jnp.concatenate([wh[at, :], ch[at, :]], axis=1)
    right_l = jnp.concatenate([wl[at, :], cl[at, :]], axis=1)
    for i in range(4):
        rows = slice(i * 256, i * 256 + 256)
        out[rows, :] = a[rows, :] - dot3(
            (lh[rows, :], ll[rows, :]), (right_h, right_l), NT
        )


def update(tab, matrix, pieces, ch, cl, rh, rl, oh, ol):
    return pl.pallas_call(
        update_kernel,
        grid_spec=pltpu.PrefetchScalarGridSpec(
            num_scalar_prefetch=1,
            grid=(8,),
            in_specs=[pl.BlockSpec((1024, 256), lambda s, t: (0, s))]
            + [full((1024, 256))] * 4
            + [full((2048, 512))] * 2
            + [full((1024, 512))] * 4,
            out_specs=pl.BlockSpec((1024, 256), lambda s, t: (0, s)),
            scratch_shapes=[pltpu.VMEM((2048, 512), BF16)] * 2
            + [pltpu.VMEM((1024, 1024), BF16)] * 2,
        ),
        out_shape=jax.ShapeDtypeStruct((1024, 2048), F32),
        compiler_params=params(50),
        cost_estimate=cost(2 * 1024 * 2048 * 512, 28 << 20),
    )(tab, matrix, *pieces, ch, cl, rh, rl, oh, ol)


def basis_update_kernel(tab, b_ref, p0, p1, p2, p3, rh, rl, out, qh, ql):
    place_blocks(tab, (p0, p1, p2, p3), qh, ql, 32)
    out[...] = b_ref[...] - dot3((qh[...], ql[...]), (rh[...], rl[...]), NT)


def basis_update(tab, basis, pieces, rh, rl):
    return pl.pallas_call(
        basis_update_kernel,
        grid_spec=pltpu.PrefetchScalarGridSpec(
            num_scalar_prefetch=1,
            grid=(1,),
            in_specs=[full((512, 1024))]
            + [full((256, 256))] * 4
            + [full((1024, 512))] * 2,
            out_specs=full((512, 1024)),
            scratch_shapes=[pltpu.VMEM((512, 512), BF16)] * 2,
        ),
        out_shape=jax.ShapeDtypeStruct((512, 1024), F32),
        compiler_params=params(32),
        cost_estimate=cost(512 * 1024 * 512, 7 << 20),
    )(tab, basis, *pieces, rh, rl)


def on_device(matrix, basis_rows, reflectors, tfactor):
    dev = lax.axis_index(EVERY)
    tab = lax.dynamic_index_in_dim(jnp.asarray(TABLES), dev, 0, keepdims=False)
    own_v = lax.dynamic_slice_in_dim(reflectors, tab[40] * 128, 128, 0)

    q = list(basis_product(tab, basis_rows, reflectors))
    v = [own_v[:, :256], own_v[:, 256:]]
    last_v = [None, None]
    for s in range(4):
        for h in range(2):
            half = q[h].shape[0] // 2
            message = jnp.concatenate([v[h], q[h][half:]], axis=0)
            got = moved(message, lambda c: row_dim(c, h, s))
            n = v[h].shape[0]
            q[h] = q[h][:half] + got[n:]
            if s < 3:
                v[h] = jnp.concatenate([v[h], got[:n]], axis=0)
            else:
                last_v[h] = got[:n]
    v_pieces = (v[0], last_v[0], v[1], last_v[1])

    send, keep = apply_matrix(tab, matrix, v_pieces)
    w = keep + moved(send, lambda c: "c")
    g_send, g_keep = inner_product(tab, reflectors, send, keep)
    g = g_keep + moved(g_send, lambda c: "c")
    w, g = w.reshape(4, 128, 512), g.reshape(4, 64, 512)
    for s in range(2):
        w = w.reshape(-1, 2, 128, 512)
        g = g.reshape(-1, 2, 64, 512)
        n = w.shape[0]
        message = jnp.concatenate(
            [w[:, 1].reshape(n * 128, 512), g[:, 1].reshape(n * 64, 512)], axis=0
        )
        got = moved(message, lambda c: y_dim(c, s))
        w = w[:, 0] + got[: n * 128].reshape(n, 128, 512)
        g = g[:, 0] + got[n * 128 :].reshape(n, 64, 512)
    w, g = w.reshape(128, 512), g.reshape(64, 512)

    ch, cl, rh, rl = turned(tab, tfactor, reflectors, v_pieces)

    wc = [w[:, :256], w[:, 256:]]
    last_w, last_q = [None, None], [None, None]
    w_rows = w
    for s in range(4):
        g = g + moved(g, lambda c: row_dim(c, 0, s))
        for h in range(2):
            n = wc[h].shape[0]
            got = moved(
                jnp.concatenate([wc[h], q[h]], axis=0), lambda c: row_dim(c, h, s)
            )
            if s < 3:
                wc[h] = jnp.concatenate([wc[h], got[:n]], axis=0)
                q[h] = jnp.concatenate([q[h], got[n:]], axis=0)
            else:
                last_w[h], last_q[h] = got[:n], got[n:]
        if s < 2:
            w_rows = jnp.concatenate(
                [w_rows, moved(w_rows, lambda c: y_dim(c, s))], axis=0
            )
    w_other = moved(w_rows, lambda c: "c")
    for s in range(2):
        g = jnp.concatenate([g, moved(g, lambda c: y_dim(c, s))], axis=0)
    g_other = moved(g, lambda c: "c")

    new_basis = basis_update(tab, basis_rows, (q[0], last_q[0], q[1], last_q[1]), rh, rl)
    oh, ol = rows_less(tab, w_rows, w_other, g, g_other, rh, rl)
    new_matrix = update(
        tab, matrix, (wc[0], last_w[0], wc[1], last_w[1]), ch, cl, rh, rl, oh, ol
    )
    return new_matrix, new_basis


def solution(mesh):
    placed = (P("row", ("col", "grp")), P(("col", "grp"), "row"), P("row", None), P())
    return jax.shard_map(
        on_device,
        mesh=mesh,
        in_specs=placed,
        out_specs=(P("row", ("col", "grp")), P(("col", "grp"), "row")),
        check_vma=False,
    )
```

profile of v0, /device:TPU:0, one launch (start us, length us, event | category | flops | bytes accessed | tf_op | source)
XLA Modules:
  0.0 185.5 jit_solution(10627320926303753131)
XLA Ops:
  12.1 4.1 %collective-permute-done.4 = f32[384,256]{1,0:T(8,128)S(1)} collective-permute-done((f32[384,256]{1,0:T(8,128)S(1)}, f32[384,256]{1,0:T(8,128)S(1)}, u32[]{:S(2)}, u32[]{:S(2)}) %collective-permute-start.4) | collective-permute-done | bytes 393248 | tf_op jit(solution)/shard_map/ppermute | solution.py:86
  16.3 2.9 %collective-permute-start.5 = (f32[384,256]{1,0:T(8,128)S(1)}, f32[384,256]{1,0:T(8,128)S(1)}, u32[]{:S(2)}, u32[]{:S(2)}) collective-permute-start(f32[384,256]{1,0:T(8,128)S(1)} %fusion.1), channel_id=1, source_target_pairs={{0,96},{1,97},{2,34},{3,35},{4,100},{5,101},{6,38},{7,39},{8,104},... | collective-permute-start | bytes 1179656 | tf_op jit(solution)/shard_map/ppermute | solution.py:86
  21.4 4.0 %collective-permute-done.5 = f32[384,256]{1,0:T(8,128)S(1)} collective-permute-done((f32[384,256]{1,0:T(8,128)S(1)}, f32[384,256]{1,0:T(8,128)S(1)}, u32[]{:S(2)}, u32[]{:S(2)}) %collective-permute-start.5) | collective-permute-done | bytes 393248 | tf_op jit(solution)/shard_map/ppermute | solution.py:86
  25.5 4.2 %collective-permute-start.6 = (f32[576,256]{1,0:T(8,128)S(1)}, f32[576,256]{1,0:T(8,128)S(1)}, u32[]{:S(2)}, u32[]{:S(2)}) collective-permute-start(f32[576,256]{1,0:T(8,128)S(1)} %pad_maximum_fusion.7), channel_id=1, source_target_pairs={{0,24},{1,25},{2,10},{3,11},{4,28},{5,29},{6,14},{7,15},{8,16},{9,... | collective-permute-start | bytes 1769480 | tf_op jit(solution)/shard_map/ppermute | solution.py:86
  29.9 2.8 %collective-permute-start.2 = (f32[576,256]{1,0:T(8,128)S(1)}, f32[576,256]{1,0:T(8,128)S(1)}, u32[]{:S(2)}, u32[]{:S(2)}) collective-permute-start(f32[576,256]{1,0:T(8,128)S(1)} %pad_maximum_fusion.6), channel_id=1, source_target_pairs={{0,96},{1,97},{2,34},{3,35},{4,100},{5,101},{6,38},{7,39},{8,104},... | collective-permute-start | bytes 1769480 | tf_op jit(solution)/shard_map/ppermute | solution.py:86
  32.7 4.9 %collective-permute-done.6 = f32[576,256]{1,0:T(8,128)S(1)} collective-permute-done((f32[576,256]{1,0:T(8,128)S(1)}, f32[576,256]{1,0:T(8,128)S(1)}, u32[]{:S(2)}, u32[]{:S(2)}) %collective-permute-start.6) | collective-permute-done | bytes 589856 | tf_op jit(solution)/shard_map/ppermute | solution.py:86
  38.0 6.3 %collective-permute-done.2 = f32[576,256]{1,0:T(8,128)S(1)} collective-permute-done((f32[576,256]{1,0:T(8,128)S(1)}, f32[576,256]{1,0:T(8,128)S(1)}, u32[]{:S(2)}, u32[]{:S(2)}) %collective-permute-start.2) | collective-permute-done | bytes 589856 | tf_op jit(solution)/shard_map/ppermute | solution.py:86
  46.0 6.9 %collective-permute-done.7 = f32[1056,256]{1,0:T(8,128)S(1)} collective-permute-done((f32[1056,256]{1,0:T(8,128)S(1)}, f32[1056,256]{1,0:T(8,128)S(1)}, u32[]{:S(2)}, u32[]{:S(2)}) %collective-permute-start.7) | collective-permute-done | bytes 1081376 | tf_op jit(solution)/shard_map/ppermute | solution.py:86
  53.0 8.1 %collective-permute-done.3 = f32[1056,256]{1,0:T(8,128)S(1)} collective-permute-done((f32[1056,256]{1,0:T(8,128)S(1)}, f32[1056,256]{1,0:T(8,128)S(1)}, u32[]{:S(2)}, u32[]{:S(2)}) %collective-permute-start.3) | collective-permute-done | bytes 1081376 | tf_op jit(solution)/shard_map/ppermute | solution.py:86
  61.1 10.6 %shard_map.69 = (f32[512,512]{1,0:T(8,128)S(1)}, f32[512,512]{1,0:T(8,128)S(1)}) custom-call(s32[64]{0:T(128)S(1)} %get-tuple-element.75.tab, f32[1024,2048]{1,0:T(8,128)} %a.1, f32[1024,2048]{1,0:T(8,128)} %a.1, f32[1024,2048]{1,0:T(8,128)} %a.1, f32[1024,2048]{1,0:T(8,128)} %a.1, f32[1024,256]{1,0:T(8,128)S(1)} %pad_maximum_fusion.p0, ...), custom_call_target="tpu_custom_call" | custom-call | flops 6442450944 | bytes 14680064 | tf_op jit(solution)/shard_map/pallas_call | solution.py:175
  71.8 2.5 %shard_map.70 = (f32[256,512]{1,0:T(8,128)S(1)}, f32[256,512]{1,0:T(8,128)S(1)}) custom-call(s32[64]{0:T(128)S(1)} %get-tuple-element.75.tab, f32[1024,512]{1,0:T(8,128)S(1)} %copy-done.7, f32[512,512]{1,0:T(8,128)S(1)} %get-tuple-element.17.s_ref, f32[512,512]{1,0:T(8,128)S(1)} %get-tuple-element.16.k_ref), custom_call_target="tpu_custom_call" | custom-call | flops 1610612736 | bytes 5242880 | tf_op jit(solution)/shard_map/pallas_call | solution.py:208
  78.5 10.4 %collective-permute-done.10 = f32[384,512]{1,0:T(8,128)S(1)} collective-permute-done((f32[384,512]{1,0:T(8,128)S(1)}, f32[384,512]{1,0:T(8,128)S(1)}, u32[]{:S(2)}, u32[]{:S(2)}) %collective-permute-start.10) | collective-permute-done | bytes 786464 | tf_op jit(solution)/shard_map/ppermute | solution.py:86
  89.2 3.1 %collective-permute-start.11 = (f32[192,512]{1,0:T(8,128)S(1)}, f32[192,512]{1,0:T(8,128)S(1)}, u32[]{:S(2)}, u32[]{:S(2)}) collective-permute-start(f32[192,512]{1,0:T(8,128)S(1)} %pad_maximum_fusion.14), channel_id=1, source_target_pairs={{0,5},{1,4},{2,6},{3,7},{4,1},{5,0},{6,2},{7,3},{8,13},{9,12},{10,... | collective-permute-start | bytes 1179656 | tf_op jit(solution)/shard_map/ppermute | solution.py:86
  92.3 6.0 %collective-permute-done.11 = f32[192,512]{1,0:T(8,128)S(1)} collective-permute-done((f32[192,512]{1,0:T(8,128)S(1)}, f32[192,512]{1,0:T(8,128)S(1)}, u32[]{:S(2)}, u32[]{:S(2)}) %collective-permute-start.11) | collective-permute-done | bytes 393248 | tf_op jit(solution)/shard_map/ppermute | solution.py:86
  105.3 2.9 %collective-permute-start.17 = (f32[320,256]{1,0:T(8,128)S(1)}, f32[320,256]{1,0:T(8,128)S(1)}, u32[]{:S(2)}, u32[]{:S(2)}) collective-permute-start(f32[320,256]{1,0:T(8,128)S(1)} %pad_maximum_fusion.16), channel_id=1, source_target_pairs={{0,96},{1,97},{2,34},{3,35},{4,100},{5,101},{6,38},{7,39},{8,104},... | collective-permute-start | bytes 983048 | tf_op jit(solution)/shard_map/ppermute | solution.py:86
  108.7 2.9 %collective-permute-start.25 = (f32[64,512]{1,0:T(8,128)S(1)}, f32[64,512]{1,0:T(8,128)S(1)}, u32[]{:S(2)}, u32[]{:S(2)}) collective-permute-start(f32[64,512]{1,0:T(8,128)S(1)} %add.102), channel_id=1, source_target_pairs={{0,96},{1,97},{2,34},{3,35},{4,100},{5,101},{6,38},{7,39},{8,104},... | collective-permute-start | bytes 393224 | tf_op jit(solution)/shard_map/ppermute | solution.py:86
  117.3 3.5 %collective-permute-done.13 = f32[320,256]{1,0:T(8,128)S(1)} collective-permute-done((f32[320,256]{1,0:T(8,128)S(1)}, f32[320,256]{1,0:T(8,128)S(1)}, u32[]{:S(2)}, u32[]{:S(2)}) %collective-permute-start.13) | collective-permute-done | bytes 327712 | tf_op jit(solution)/shard_map/ppermute | solution.py:86
  124.3 3.1 %collective-permute-start.21 = (f32[256,512]{1,0:T(8,128)S(1)}, f32[256,512]{1,0:T(8,128)S(1)}, u32[]{:S(2)}, u32[]{:S(2)}) collective-permute-start(f32[256,512]{1,0:T(8,128)S(1)} %pad_maximum_fusion.8), channel_id=1, source_target_pairs={{0,5},{1,4},{2,6},{3,7},{4,1},{5,0},{6,2},{7,3},{8,13},{9,12},{10,... | collective-permute-start | bytes 1572872 | tf_op jit(solution)/shard_map/ppermute | solution.py:86
  129.5 3.5 %collective-permute-start.28 = (f32[128,512]{1,0:T(8,128)S(1)}, f32[128,512]{1,0:T(8,128)S(1)}, u32[]{:S(2)}, u32[]{:S(2)}) collective-permute-start(f32[128,512]{1,0:T(8,128)S(1)} %pad_maximum_fusion.17), channel_id=1, source_target_pairs={{0,5},{1,4},{2,6},{3,7},{4,1},{5,0},{6,2},{7,3},{8,13},{9,12},{10,... | collective-permute-start | bytes 786440 | tf_op jit(solution)/shard_map/ppermute | solution.py:86
  142.9 8.8 %shard_map.71 = (bf16[2048,512]{1,0:T(8,128)(2,1)}, bf16[2048,512]{1,0:T(8,128)(2,1)}, bf16[1024,512]{1,0:T(8,128)(2,1)S(1)}, bf16[1024,512]{1,0:T(8,128)(2,1)S(1)}) custom-call(s32[64]{0:T(128)S(1)} %get-tuple-element.75.tab, f32[512,512]{1,0:T(8,128)S(1)} %copy-done.8, f32[1024,512]{1,0:T(8,128)} %v_ref.5, f32[1024,256]{1,0:T(8,128)S(1)} %pad_maximum_fusion.p0, ...), custom_call_target="tpu_custom_call" | custom-call | flops 4831838208 | bytes 13631488 | tf_op jit(solution)/shard_map/pallas_call | solution.py:235
  152.0 2.6 %shard_map.72 = (bf16[1024,512]{1,0:T(8,128)(2,1)S(1)}, bf16[1024,512]{1,0:T(8,128)(2,1)S(1)}) custom-call(s32[64]{0:T(128)S(1)} %get-tuple-element.75.tab, f32[512,512]{1,0:T(8,128)S(1)} %pad_maximum_fusion.4.wk_ref, f32[512,512]{1,0:T(8,128)S(1)} %collective-permute-done.22.ws_ref, f32[256,512]{1,0:T(8,128)S(1)} %pad_maximum_fusion.9.gk_ref, ...), custom_call_target="tpu_custom_call" | custom-call | flops 1610612736 | bytes 7340032 | tf_op jit(solution)/shard_map/pallas_call | solution.py:267
  156.2 3.1 %collective-permute-done.15 = f32[1280,256]{1,0:T(8,128)S(1)} collective-permute-done((f32[1280,256]{1,0:T(8,128)}, f32[1280,256]{1,0:T(8,128)S(1)}, u32[]{:S(2)}, u32[]{:S(2)}) %collective-permute-start.15) | collective-permute-done | bytes 1310752 | tf_op jit(solution)/shard_map/ppermute | solution.py:86
  159.4 3.8 %shard_map.74 = f32[512,1024]{1,0:T(8,128)} custom-call(s32[64]{0:T(128)S(1)} %get-tuple-element.75.tab, f32[512,1024]{1,0:T(8,128)S(1)} %copy-done.3, f32[256,256]{1,0:T(8,128)S(1)} %pad_maximum_fusion.18.p0, f32[256,256]{1,0:T(8,128)S(1)} %slice.317.p1, f32[256,256]{1,0:T(8,128)S(1)} %pad_maximum_fusion.19.p2, f32[256,256]{1,0:T(8,128)S(1)} %slice.318.p3, ...), custom_call_target="tpu_custom_call" | custom-call | flops 1610612736 | bytes 7340032 | tf_op jit(solution)/shard_map/pallas_call | solution.py:331
  164.3 21.2 %shard_map.73 = f32[1024,2048]{1,0:T(8,128)} custom-call(s32[64]{0:T(128)S(1)} %get-tuple-element.75.tab, f32[1024,2048]{1,0:T(8,128)} %a.1, f32[1024,256]{1,0:T(8,128)S(1)} %pad_maximum_fusion.2.p0, f32[1024,256]{1,0:T(8,128)S(1)} %slice.304.p1, f32[1024,256]{1,0:T(8,128)S(1)} %pad_maximum_fusion.3.p2, f32[1024,256]{1,0:T(8,128)} %slice.314.p3, ...), custom_call_target="tpu_custom_call" | custom-call | flops 12884901888 | bytes 29360128 | tf_op jit(solution)/shard_map/pallas_call | solution.py:306
  (157 shorter events, 51.4 us)
Async XLA Ops:
  8.3 7.9 %collective-permute-start.4 = (f32[384,256]{1,0:T(8,128)S(1)}, f32[384,256]{1,0:T(8,128)S(1)}, u32[]{:S(2)}, u32[]{:S(2)}) collective-permute-start(f32[384,256]{1,0:T(8,128)S(1)} %pad_maximum_fusion.13), channel_id=1, source_target_pairs={{0,8},{1,9},{2,26},{3,27},{4,12},{5,13},{6,30},{7,31},{8,0},{9,1},... | collective-permute-start | bytes 1179656 | tf_op jit(solution)/shard_map/ppermute | solution.py:86
  10.5 8.8 %collective-permute-start = (f32[384,256]{1,0:T(8,128)S(1)}, f32[384,256]{1,0:T(8,128)S(1)}, u32[]{:S(2)}, u32[]{:S(2)}) collective-permute-start(f32[384,256]{1,0:T(8,128)S(1)} %pad_maximum_fusion.11), channel_id=1, source_target_pairs={{0,32},{1,33},{2,98},{3,99},{4,36},{5,37},{6,102},{7,103},{8,40},{... | collective-permute-start | bytes 1179656 | tf_op jit(solution)/shard_map/ppermute | solution.py:86
  16.3 9.1 %collective-permute-start.5 = (f32[384,256]{1,0:T(8,128)S(1)}, f32[384,256]{1,0:T(8,128)S(1)}, u32[]{:S(2)}, u32[]{:S(2)}) collective-permute-start(f32[384,256]{1,0:T(8,128)S(1)} %fusion.1), channel_id=1, source_target_pairs={{0,96},{1,97},{2,34},{3,35},{4,100},{5,101},{6,38},{7,39},{8,104},... | collective-permute-start | bytes 1179656 | tf_op jit(solution)/shard_map/ppermute | solution.py:86
  19.4 10.3 %collective-permute-start.1 = (f32[384,256]{1,0:T(8,128)S(1)}, f32[384,256]{1,0:T(8,128)S(1)}, u32[]{:S(2)}, u32[]{:S(2)}) collective-permute-start(f32[384,256]{1,0:T(8,128)S(1)} %fusion.2), channel_id=1, source_target_pairs={{0,8},{1,9},{2,26},{3,27},{4,12},{5,13},{6,30},{7,31},{8,0},{9,1},... | collective-permute-start | bytes 1179656 | tf_op jit(solution)/shard_map/ppermute | solution.py:86
  25.5 12.1 %collective-permute-start.6 = (f32[576,256]{1,0:T(8,128)S(1)}, f32[576,256]{1,0:T(8,128)S(1)}, u32[]{:S(2)}, u32[]{:S(2)}) collective-permute-start(f32[576,256]{1,0:T(8,128)S(1)} %pad_maximum_fusion.7), channel_id=1, source_target_pairs={{0,24},{1,25},{2,10},{3,11},{4,28},{5,29},{6,14},{7,15},{8,16},{9,... | collective-permute-start | bytes 1769480 | tf_op jit(solution)/shard_map/ppermute | solution.py:86
  29.9 14.5 %collective-permute-start.2 = (f32[576,256]{1,0:T(8,128)S(1)}, f32[576,256]{1,0:T(8,128)S(1)}, u32[]{:S(2)}, u32[]{:S(2)}) collective-permute-start(f32[576,256]{1,0:T(8,128)S(1)} %pad_maximum_fusion.6), channel_id=1, source_target_pairs={{0,96},{1,97},{2,34},{3,35},{4,100},{5,101},{6,38},{7,39},{8,104},... | collective-permute-start | bytes 1769480 | tf_op jit(solution)/shard_map/ppermute | solution.py:86
  37.7 15.2 %collective-permute-start.7 = (f32[1056,256]{1,0:T(8,128)S(1)}, f32[1056,256]{1,0:T(8,128)S(1)}, u32[]{:S(2)}, u32[]{:S(2)}) collective-permute-start(f32[1056,256]{1,0:T(8,128)S(1)} %constant_dynamic-update-slice_fusion.5), channel_id=1, source_target_pairs={{0,32},{1,33},{2,98},{3,99},{4,36},{5,37},{6,102},{7,103},{8,40},{... | collective-permute-start | bytes 3244040 | tf_op jit(solution)/shard_map/ppermute | solution.py:86
  44.4 16.6 %collective-permute-start.3 = (f32[1056,256]{1,0:T(8,128)S(1)}, f32[1056,256]{1,0:T(8,128)S(1)}, u32[]{:S(2)}, u32[]{:S(2)}) collective-permute-start(f32[1056,256]{1,0:T(8,128)S(1)} %constant_dynamic-update-slice_fusion), channel_id=1, source_target_pairs={{0,24},{1,25},{2,10},{3,11},{4,28},{5,29},{6,14},{7,15},{8,16},{9,... | collective-permute-start | bytes 3244040 | tf_op jit(solution)/shard_map/ppermute | solution.py:86
  76.9 12.1 %collective-permute-start.10 = (f32[384,512]{1,0:T(8,128)S(1)}, f32[384,512]{1,0:T(8,128)S(1)}, u32[]{:S(2)}, u32[]{:S(2)}) collective-permute-start(f32[384,512]{1,0:T(8,128)S(1)} %pad_maximum_fusion.5), channel_id=1, source_target_pairs={{0,4},{1,5},{2,7},{3,6},{4,0},{5,1},{6,3},{7,2},{8,12},{9,13},{10,... | collective-permute-start | bytes 2359304 | tf_op jit(solution)/shard_map/ppermute | solution.py:86
  89.2 9.1 %collective-permute-start.11 = (f32[192,512]{1,0:T(8,128)S(1)}, f32[192,512]{1,0:T(8,128)S(1)}, u32[]{:S(2)}, u32[]{:S(2)}) collective-permute-start(f32[192,512]{1,0:T(8,128)S(1)} %pad_maximum_fusion.14), channel_id=1, source_target_pairs={{0,5},{1,4},{2,6},{3,7},{4,1},{5,0},{6,2},{7,3},{8,13},{9,12},{10,... | collective-permute-start | bytes 1179656 | tf_op jit(solution)/shard_map/ppermute | solution.py:86
  99.3 24.9 %collective-permute-start.20 = (f32[128,512]{1,0:T(8,128)S(1)}, f32[128,512]{1,0:T(8,128)S(1)}, u32[]{:S(2)}, u32[]{:S(2)}) collective-permute-start(f32[128,512]{1,0:T(8,128)S(1)} %slice_add_fusion), channel_id=1, source_target_pairs={{0,4},{1,5},{2,7},{3,6},{4,0},{5,1},{6,3},{7,2},{8,12},{9,13},{10,... | collective-permute-start | bytes 786440 | tf_op jit(solution)/shard_map/ppermute | solution.py:86
  99.8 11.8 %collective-permute-start.12 = (f32[160,256]{1,0:T(8,128)S(1)}, f32[160,256]{1,0:T(8,128)S(1)}, u32[]{:S(2)}, u32[]{:S(2)}) collective-permute-start(f32[160,256]{1,0:T(8,128)S(1)} %pad_maximum_fusion.20), channel_id=1, source_target_pairs={{0,32},{1,33},{2,98},{3,99},{4,36},{5,37},{6,102},{7,103},{8,40},{... | collective-permute-start | bytes 491528 | tf_op jit(solution)/shard_map/ppermute | solution.py:86
  105.3 11.2 %collective-permute-start.17 = (f32[320,256]{1,0:T(8,128)S(1)}, f32[320,256]{1,0:T(8,128)S(1)}, u32[]{:S(2)}, u32[]{:S(2)}) collective-permute-start(f32[320,256]{1,0:T(8,128)S(1)} %pad_maximum_fusion.16), channel_id=1, source_target_pairs={{0,96},{1,97},{2,34},{3,35},{4,100},{5,101},{6,38},{7,39},{8,104},... | collective-permute-start | bytes 983048 | tf_op jit(solution)/shard_map/ppermute | solution.py:86
  112.3 8.6 %collective-permute-start.13 = (f32[320,256]{1,0:T(8,128)S(1)}, f32[320,256]{1,0:T(8,128)S(1)}, u32[]{:S(2)}, u32[]{:S(2)}) collective-permute-start(f32[320,256]{1,0:T(8,128)S(1)} %pad_maximum_fusion.15), channel_id=1, source_target_pairs={{0,8},{1,9},{2,26},{3,27},{4,12},{5,13},{6,30},{7,31},{8,0},{9,1},... | collective-permute-start | bytes 983048 | tf_op jit(solution)/shard_map/ppermute | solution.py:86
  115.1 7.9 %collective-permute-start.26 = (f32[64,512]{1,0:T(8,128)S(1)}, f32[64,512]{1,0:T(8,128)S(1)}, u32[]{:S(2)}, u32[]{:S(2)}) collective-permute-start(f32[64,512]{1,0:T(8,128)S(1)} %add.103), channel_id=1, source_target_pairs={{0,24},{1,25},{2,10},{3,11},{4,28},{5,29},{6,14},{7,15},{8,16},{9,... | collective-permute-start | bytes 393224 | tf_op jit(solution)/shard_map/ppermute | solution.py:86
  121.6 11.9 %collective-permute-start.14 = (f32[640,256]{1,0:T(8,128)S(1)}, f32[640,256]{1,0:T(8,128)S(1)}, u32[]{:S(2)}, u32[]{:S(2)}) collective-permute-start(f32[640,256]{1,0:T(8,128)S(1)} %get-tuple-element.55), channel_id=1, source_target_pairs={{0,96},{1,97},{2,34},{3,35},{4,100},{5,101},{6,38},{7,39},{8,104},... | collective-permute-start | bytes 1966088 | tf_op jit(solution)/shard_map/ppermute | solution.py:86
  121.8 13.2 %collective-permute-start.18 = (f32[640,256]{1,0:T(8,128)S(1)}, f32[640,256]{1,0:T(8,128)S(1)}, u32[]{:S(2)}, u32[]{:S(2)}) collective-permute-start(f32[640,256]{1,0:T(8,128)S(1)} %get-tuple-element.53), channel_id=1, source_target_pairs={{0,24},{1,25},{2,10},{3,11},{4,28},{5,29},{6,14},{7,15},{8,16},{9,... | collective-permute-start | bytes 1966088 | tf_op jit(solution)/shard_map/ppermute | solution.py:86
  123.0 6.5 %collective-permute-start.27 = (f32[64,512]{1,0:T(8,128)S(1)}, f32[64,512]{1,0:T(8,128)S(1)}, u32[]{:S(2)}, u32[]{:S(2)}) collective-permute-start(f32[64,512]{1,0:T(8,128)S(1)} %add.104), channel_id=1, source_target_pairs={{0,4},{1,5},{2,7},{3,6},{4,0},{5,1},{6,3},{7,2},{8,12},{9,13},{10,... | collective-permute-start | bytes 393224 | tf_op jit(solution)/shard_map/ppermute | solution.py:86
  124.3 17.8 %collective-permute-start.21 = (f32[256,512]{1,0:T(8,128)S(1)}, f32[256,512]{1,0:T(8,128)S(1)}, u32[]{:S(2)}, u32[]{:S(2)}) collective-permute-start(f32[256,512]{1,0:T(8,128)S(1)} %pad_maximum_fusion.8), channel_id=1, source_target_pairs={{0,5},{1,4},{2,6},{3,7},{4,1},{5,0},{6,2},{7,3},{8,13},{9,12},{10,... | collective-permute-start | bytes 1572872 | tf_op jit(solution)/shard_map/ppermute | solution.py:86
  129.5 12.8 %collective-permute-start.28 = (f32[128,512]{1,0:T(8,128)S(1)}, f32[128,512]{1,0:T(8,128)S(1)}, u32[]{:S(2)}, u32[]{:S(2)}) collective-permute-start(f32[128,512]{1,0:T(8,128)S(1)} %pad_maximum_fusion.17), channel_id=1, source_target_pairs={{0,5},{1,4},{2,6},{3,7},{4,1},{5,0},{6,2},{7,3},{8,13},{9,12},{10,... | collective-permute-start | bytes 786440 | tf_op jit(solution)/shard_map/ppermute | solution.py:86
  138.4 17.8 %collective-permute-start.19 = (f32[1280,256]{1,0:T(8,128)}, f32[1280,256]{1,0:T(8,128)S(1)}, u32[]{:S(2)}, u32[]{:S(2)}) collective-permute-start(f32[1280,256]{1,0:T(8,128)} %get-tuple-element.33), channel_id=1, source_target_pairs={{0,32},{1,33},{2,98},{3,99},{4,36},{5,37},{6,102},{7,103},{8,40},{... | collective-permute-start | bytes 3932168 | tf_op jit(solution)/shard_map/ppermute | solution.py:86
  140.3 19.0 %collective-permute-start.15 = (f32[1280,256]{1,0:T(8,128)}, f32[1280,256]{1,0:T(8,128)S(1)}, u32[]{:S(2)}, u32[]{:S(2)}) collective-permute-start(f32[1280,256]{1,0:T(8,128)} %get-tuple-element.35), channel_id=1, source_target_pairs={{0,24},{1,25},{2,10},{3,11},{4,28},{5,29},{6,14},{7,15},{8,16},{9,... | collective-permute-start | bytes 3932168 | tf_op jit(solution)/shard_map/ppermute | solution.py:86
  142.2 9.8 %collective-permute-start.22 = (f32[512,512]{1,0:T(8,128)S(1)}, f32[512,512]{1,0:T(8,128)S(1)}, u32[]{:S(2)}, u32[]{:S(2)}) collective-permute-start(f32[512,512]{1,0:T(8,128)S(1)} %pad_maximum_fusion.4.wk_ref), channel_id=1, source_target_pairs={{0,2},{1,3},{2,0},{3,1},{4,6},{5,7},{6,4},{7,5},{8,10},{9,11},{10,... | collective-permute-start | bytes 3145736 | tf_op jit(solution)/shard_map/ppermute | solution.py:86
  142.3 9.6 %collective-permute-start.29 = (f32[256,512]{1,0:T(8,128)S(1)}, f32[256,512]{1,0:T(8,128)S(1)}, u32[]{:S(2)}, u32[]{:S(2)}) collective-permute-start(f32[256,512]{1,0:T(8,128)S(1)} %pad_maximum_fusion.9.gk_ref), channel_id=1, source_target_pairs={{0,2},{1,3},{2,0},{3,1},{4,6},{5,7},{6,4},{7,5},{8,10},{9,11},{10,... | collective-permute-start | bytes 1572872 | tf_op jit(solution)/shard_map/ppermute | solution.py:86
  (17 other events, 111.2 us)
where the time goes:
time: 187 us; the launch traced here: 186 us
  waiting for transfers between devices  67.8 us (36%)
  Pallas kernels  51.8 us (28%)
  starting transfers between devices  45.6 us (24%)
  local copies, waits for them, and re-layouts  16.8 us (9%)
  between operations  1.95 us (1%)
    ppermute x30, waiting for transfers between devices, moved(): return lax.ppermute(x, EVERY, pairs)  67.8 us
    ppermute x30, starting transfers between devices, moved(): return lax.ppermute(x, EVERY, pairs)  45.6 us
    pallas_call x1, Pallas kernels, update(): pl.pallas_call(update_kernel, grid_spec=pltpu.PrefetchScalarGridSpec(num_...  21.2 us
    unnamed x46, local copies, waits for them, and re-layouts  12.6 us
    pallas_call x1, Pallas kernels, apply_matrix(): pl.pallas_call(apply_kernel, grid_spec=pltpu.PrefetchScalarGridSpec(num_s...  10.6 us
    pallas_call x1, Pallas kernels, turned(): pl.pallas_call(turned_kernel, grid_spec=pltpu.PrefetchScalarGridSpec(num_...  8.81 us
    pallas_call x1, Pallas kernels, basis_update(): pl.pallas_call(basis_update_kernel, grid_spec=pltpu.PrefetchScalarGridSpe...  3.77 us
  transfers between devices with their start and end apart: 30, of which 18 were waited for; matrix products, arithmetic and copies ran while one was open for 6% of the time, Pallas kernels for 7%

commit v1 on v0

v1 whole, which is shorter than its diff:
```python
import jax
import jax.numpy as jnp
import numpy as np
from jax import lax
from jax.experimental import pallas as pl
from jax.experimental.pallas import tpu as pltpu
from jax.sharding import PartitionSpec as P

F32, BF16 = jnp.float32, jnp.bfloat16
EVERY = ("row", "col", "grp")
NN = (((1,), (0,)), ((), ()))
NT = (((1,), (1,)), ((), ()))
TN = (((0,), (0,)), ((), ()))


def flip_ring(i, bit):
    g = (i ^ (i >> 1)) ^ (1 << bit)
    return g ^ (g >> 1)


def linear(x, z, y, core):
    return (x * 4 + z) * 8 + ((y % 2) * 2 + core) * 2 + y // 2


def coords(dev):
    row, member = divmod(dev, 8)
    return row // 4, row % 4, (member % 2) * 2 + member // 4, (member // 2) % 2


def flip(dev, dim):
    x, z, y, core = coords(dev)
    if dim == "c":
        return linear(x, z, y, 1 - core)
    bit = int(dim[1])
    if dim[0] == "x":
        x = flip_ring(x, bit)
    elif dim[0] == "z":
        z = flip_ring(z, bit)
    else:
        y = flip_ring(y, bit)
    return linear(x, z, y, core)


ROW_DIMS = {
    (0, 0): ("x0", "z0", "x1", "z1"),
    (1, 0): ("z0", "x0", "z1", "x1"),
    (0, 1): ("x1", "z1", "x0", "z0"),
    (1, 1): ("z1", "x1", "z0", "x0"),
}


def row_dim(core, half, step):
    return ROW_DIMS[core, half][step]


def y_dim(core, step):
    return "y%d" % ((step + core) % 2)


def relative(dev, dims, j):
    for k, dim in enumerate(dims):
        if j >> k & 1:
            dev = flip(dev, dim)
    return dev


def build_tables():
    out = np.zeros((128, 64), np.int32)
    for dev in range(128):
        core = coords(dev)[3]
        for h in range(2):
            dims = [row_dim(core, h, s) for s in range(4)]
            for j in range(16):
                out[dev, h * 16 + j] = relative(dev, dims, j) // 8
        other = flip(dev, "c")
        for first, base in ((other, 32), (dev, 36)):
            dims = [y_dim(coords(first)[3], s) for s in range(2)]
            for j in range(4):
                out[dev, base + j] = relative(first, dims, j) % 8
        out[dev, 40] = dev % 8
    return out


TABLES = build_tables()


def moved(x, dim_of_core):
    pairs = [(dev, flip(dev, dim_of_core(coords(dev)[3]))) for dev in range(128)]
    return lax.ppermute(x, EVERY, pairs)


def split(x):
    hi = x.astype(BF16)
    return hi, (x - hi.astype(F32)).astype(BF16)


def dot3(a, b, dims):
    def one(u, v):
        return lax.dot_general(u, v, dims, preferred_element_type=F32)

    return one(a[0], b[0]) + (one(a[0], b[1]) + one(a[1], b[0]))


def cost(macs, moved_bytes):
    return pl.CostEstimate(flops=6 * macs, bytes_accessed=moved_bytes, transcendentals=0)


def params(mib):
    return pltpu.CompilerParams(vmem_limit_bytes=mib * 2**20)


def in_hbm(x):
    return pltpu.with_memory_space_constraint(x, pltpu.HBM)


def in_vmem(x):
    return pltpu.with_memory_space_constraint(x, pltpu.VMEM)


WHOLE = pl.BlockSpec(memory_space=pltpu.VMEM)


def full(shape):
    return pl.BlockSpec(shape, lambda *_: (0,) * len(shape))


def tiled(shape):
    return pl.BlockSpec(shape, lambda s, t: (s, 0))


def basis_kernel(tab, b_ref, v_ref, q0_ref, q1_ref, q, vh, vl):
    step = pl.program_id(0)

    @pl.when(step == 0)
    def _():
        vh[...], vl[...] = split(v_ref[...])

    rows = pl.ds(pl.multiple_of(step * 128, 128), 128)
    q[rows, :] = dot3(split(b_ref[...]), (vh[...], vl[...]), NN)

    @pl.when(step == 3)
    def _():
        for h, out in enumerate((q0_ref, q1_ref)):
            for j in range(16):
                place = (j >> 1 & 1) * 8 + (j >> 2 & 1) * 4 + (j >> 3 & 1) * 2 + (j & 1)
                rows = pl.ds(pl.multiple_of(tab[h * 16 + j] * 32, 32), 32)
                out[place * 32 : place * 32 + 32, :] = q[rows, h * 256 : h * 256 + 256]


def basis_product(tab, basis, v):
    return pl.pallas_call(
        basis_kernel,
        grid_spec=pltpu.PrefetchScalarGridSpec(
            num_scalar_prefetch=1,
            grid=(4,),
            in_specs=[tiled((128, 1024)), full((1024, 512))],
            out_specs=[full((512, 256))] * 2,
            scratch_shapes=[pltpu.VMEM((512, 512), F32)]
            + [pltpu.VMEM((1024, 512), BF16)] * 2,
        ),
        out_shape=[jax.ShapeDtypeStruct((512, 256), F32)] * 2,
        compiler_params=params(16),
        cost_estimate=cost(512 * 1024 * 512, 5 << 20),
    )(tab, in_hbm(basis), in_hbm(v))


def place_blocks(tab, pieces, hi, lo, rows=128):
    for h in range(2):
        for j in range(16):
            src = pieces[h * 2 + j // 8]
            block = src[(j % 8) * rows : (j % 8) * rows + rows, :]
            bh, bl = split(block)
            at = pl.ds(pl.multiple_of(tab[h * 16 + j] * rows, rows), rows)
            hi[at, h * 256 : h * 256 + 256] = bh
            lo[at, h * 256 : h * 256 + 256] = bl


def apply_part(tab, first, a_refs, pieces, ah, al, vh, vl, out, add):
    @pl.when(pl.program_id(0) == 0)
    def _():
        for h in range(2):
            vh[h], vl[h] = split(pieces[h][...])

    for h in range(2):
        for i, a in enumerate(a_refs):
            for j in range(8):
                at = tab[h * 16 + first + j] * 128
                block = a[:, pl.ds(pl.multiple_of(at, 128), 128)]
                rows, lanes = slice(i * 128, i * 128 + 128), slice(j * 128, j * 128 + 128)
                ah[rows, lanes], al[rows, lanes] = split(block)
        part = dot3((ah[...], al[...]), (vh[h], vl[h]), NN)
        lanes = slice(h * 256, h * 256 + 256)
        out[:, lanes] = part if add is None else part + add[:, lanes]


def apply_first_kernel(tab, a0, a1, a2, a3, p0, p1, out, ah, al, vh, vl):
    apply_part(tab, 0, (a0, a1, a2, a3), (p0, p1), ah, al, vh, vl, out, None)


def apply_last_kernel(tab, a0, a1, a2, a3, p0, p1, acc, send, keep, ah, al, vh, vl):
    for s, out in enumerate((send, keep)):

        @pl.when(pl.program_id(0) == s)
        def _(out=out):
            apply_part(tab, 8, (a0, a1, a2, a3), (p0, p1), ah, al, vh, vl, out, acc)


def apply_matrix(tab, matrix, pieces, acc=None):
    def a_spec(i):
        return pl.BlockSpec((128, 2048), lambda s, t, i=i: (t[32 + s * 4 + i], 0))

    tile = pl.BlockSpec((512, 512), lambda s, t: (s, 0))
    last = acc is not None
    return pl.pallas_call(
        apply_last_kernel if last else apply_first_kernel,
        grid_spec=pltpu.PrefetchScalarGridSpec(
            num_scalar_prefetch=1,
            grid=(2,),
            in_specs=[a_spec(i) for i in range(4)]
            + [full((1024, 256))] * 2
            + [tile] * last,
            out_specs=[full((512, 512))] * 2 if last else tile,
            scratch_shapes=[pltpu.VMEM((512, 1024), BF16)] * 2
            + [pltpu.VMEM((2, 1024, 256), BF16)] * 2,
        ),
        out_shape=[jax.ShapeDtypeStruct((512, 512), F32)] * 2
        if last
        else jax.ShapeDtypeStruct((1024, 512), F32),
        compiler_params=params(28),
        cost_estimate=cost(1024 * 1024 * 512, 12 << 20),
    )(tab, *[matrix] * 4, *pieces, *([acc] if last else []))


def inner_kernel(tab, v_ref, s_ref, k_ref, gs_ref, gk_ref, g):
    total = None
    for base, src in ((32, s_ref), (36, k_ref)):
        rows = [
            v_ref[pl.ds(pl.multiple_of(tab[base + i] * 128, 128), 128), :]
            for i in range(4)
        ]
        v = jnp.concatenate(rows, axis=0)
        part = dot3(split(v), split(src[...]), TN)
        total = part if total is None else total + part
    g[...] = total
    for base, out in ((32, gs_ref), (36, gk_ref)):
        for i in range(4):
            at = pl.ds(pl.multiple_of(tab[base + i] * 64, 64), 64)
            out[i * 64 : i * 64 + 64, :] = g[at, :]


def inner_product(tab, v, send, keep):
    return pl.pallas_call(
        inner_kernel,
        grid_spec=pltpu.PrefetchScalarGridSpec(
            num_scalar_prefetch=1,
            grid=(1,),
            in_specs=[full((1024, 512)), full((512, 512)), full((512, 512))],
            out_specs=[full((256, 512))] * 2,
            scratch_shapes=[pltpu.VMEM((512, 512), F32)],
        ),
        out_shape=[jax.ShapeDtypeStruct((256, 512), F32)] * 2,
        compiler_params=params(32),
        cost_estimate=cost(1024 * 512 * 512, 5 << 20),
    )(tab, v, send, keep)


def turned_kernel(tab, t_ref, v_ref, p0, p1, p2, p3, ch, cl, rh, rl, vh, vl):
    t = split(t_ref[...])
    place_blocks(tab, (p0, p1, p2, p3), vh, vl)
    for i in range(4):
        at = slice(i * 512, i * 512 + 512)
        ch[at, :], cl[at, :] = split(dot3((vh[at, :], vl[at, :]), t, NT))
    for i in range(2):
        at = slice(i * 512, i * 512 + 512)
        rh[at, :], rl[at, :] = split(dot3(split(v_ref[at, :]), t, NT))


def turned(tab, tfactor, v, pieces):
    return pl.pallas_call(
        turned_kernel,
        grid_spec=pltpu.PrefetchScalarGridSpec(
            num_scalar_prefetch=1,
            grid=(1,),
            in_specs=[full((512, 512)), full((1024, 512))] + [full((1024, 256))] * 4,
            out_specs=[full((2048, 512))] * 2 + [full((1024, 512))] * 2,
            scratch_shapes=[pltpu.VMEM((2048, 512), BF16)] * 2,
        ),
        out_shape=[jax.ShapeDtypeStruct((2048, 512), BF16)] * 2
        + [jax.ShapeDtypeStruct((1024, 512), BF16)] * 2,
        compiler_params=params(40),
        cost_estimate=cost(3072 * 512 * 512, 13 << 20),
    )(tab, tfactor, v, *pieces)


def place_cat(pieces, b3):
    for h, piece in enumerate(pieces):
        bh, bl = split(piece[...])
        b3[h, :, :256] = bh
        b3[h, :, 256:512] = bl
        b3[h, :, 512:] = bh


def less_blocks(tab, first, out, x, b3):
    for h in range(2):
        cols = slice(h * 256, h * 256 + 256)
        left = jnp.concatenate([x[0][:, cols], x[0][:, cols], x[1][:, cols]], axis=1)
        for p in range(4):
            right = b3[h, p * 256 : p * 256 + 256, :]
            part = lax.dot_general(left, right, NT, preferred_element_type=F32)
            for e in range(2):
                at = tab[h * 16 + first + p * 2 + e] * 128
                at = pl.ds(pl.multiple_of(at, 128), 128)
                out[:, at] = out[:, at] - part[:, e * 128 : e * 128 + 128]


def update_first_kernel(
    tab, a, p0, p1, wk, ws, gk, gs, rh, rl, ch, cl, out, b3, w, g, gh, gl
):
    step = pl.program_id(0)

    @pl.when(step == 0)
    def _():
        place_cat((p0, p1), b3)
        for base, gsrc, wsrc in ((36, gk, wk), (32, gs, ws)):
            for i in range(4):
                at = pl.ds(pl.multiple_of(tab[base + i] * 64, 64), 64)
                g[at, :] = gsrc[i * 64 : i * 64 + 64, :]
                at = pl.ds(pl.multiple_of(tab[base + i] * 128, 128), 128)
                w[at, :] = wsrc[i * 128 : i * 128 + 128, :]
        gh[...], gl[...] = split(g[...])

    x = (rh[...], rl[...])
    rows = pl.ds(pl.multiple_of(step * 256, 256), 256)
    left = split(w[rows, :] - dot3(x, (gh[...], gl[...]), NN))
    for i in range(4):
        at = slice(i * 512, i * 512 + 512)
        out[:, at] = a[:, at] - dot3(left, (ch[at, :], cl[at, :]), NT)
    less_blocks(tab, 0, out, x, b3)


def update_last_kernel(
    tab, a, p0, p1, rh, rl, b_ref, q0, q1, q2, q3, xh, xl, out, b_out,
    b3, qh, ql,
):
    step = pl.program_id(0)

    @pl.when(step == 0)
    def _():
        place_cat((p0, p1), b3)
        place_blocks(tab, (q0, q1, q2, q3), qh, ql, 32)

    out[...] = a[...]
    less_blocks(tab, 8, out, (rh[...], rl[...]), b3)
    rows = pl.ds(pl.multiple_of(step * 128, 128), 128)
    b_out[...] = b_ref[...] - dot3((qh[rows, :], ql[rows, :]), (xh[...], xl[...]), NT)


def update_first(tab, matrix, pieces, w_keep, w_other, g_keep, g_other, rh, rl, ch, cl):
    return pl.pallas_call(
        update_first_kernel,
        grid_spec=pltpu.PrefetchScalarGridSpec(
            num_scalar_prefetch=1,
            grid=(4,),
            in_specs=[tiled((256, 2048))]
            + [WHOLE] * 6
            + [tiled((256, 512))] * 2
            + [WHOLE] * 2,
            out_specs=tiled((256, 2048)),
            scratch_shapes=[pltpu.VMEM((2, 1024, 768), BF16)]
            + [pltpu.VMEM((1024, 512), F32), pltpu.VMEM((512, 512), F32)]
            + [pltpu.VMEM((512, 512), BF16)] * 2,
        ),
        out_shape=pltpu.HBM((1024, 2048), F32),
        compiler_params=params(26),
        cost_estimate=cost(7 * 1024 * 512 * 512, 26 << 20),
    )(
        tab, in_hbm(matrix),
        *[in_vmem(x) for x in (*pieces, w_keep, w_other, g_keep, g_other)],
        rh, rl, in_vmem(ch), in_vmem(cl),
    )


def update_last(tab, acc, pieces, basis, q_pieces, rh, rl):
    return pl.pallas_call(
        update_last_kernel,
        grid_spec=pltpu.PrefetchScalarGridSpec(
            num_scalar_prefetch=1,
            grid=(4,),
            in_specs=[tiled((256, 2048))]
            + [full((1024, 256))] * 2
            + [tiled((256, 512))] * 2
            + [tiled((128, 1024))]
            + [full((256, 256))] * 4
            + [full((1024, 512))] * 2,
            out_specs=[tiled((256, 2048)), tiled((128, 1024))],
            scratch_shapes=[pltpu.VMEM((2, 1024, 768), BF16)]
            + [pltpu.VMEM((512, 512), BF16)] * 2,
        ),
        out_shape=[
            jax.ShapeDtypeStruct((1024, 2048), F32),
            jax.ShapeDtypeStruct((512, 1024), F32),
        ],
        compiler_params=params(28),
        cost_estimate=cost(3 * 1024 * 512 * 512, 26 << 20),
    )(tab, in_hbm(acc), *pieces, rh, rl, in_hbm(basis), *q_pieces, rh, rl)


def on_device(matrix, basis_rows, reflectors, tfactor):
    dev = lax.axis_index(EVERY)
    tab = lax.dynamic_index_in_dim(jnp.asarray(TABLES), dev, 0, keepdims=False)
    member = lax.axis_index(("col", "grp"))
    own_v = lax.dynamic_slice_in_dim(reflectors, member * 128, 128, 0)

    q = list(basis_product(tab, basis_rows, reflectors))
    v = [own_v[:, :256], own_v[:, 256:]]
    last_v = [None, None]
    for s in range(4):
        messages = list(v)
        if s > 0:
            for h in range(2):
                half = q[h].shape[0] // 2
                messages[h] = jnp.concatenate([v[h], q[h][half:]], axis=0)
        messages = lax.optimization_barrier(messages)
        for h in range(2):
            n, half = v[h].shape[0], q[h].shape[0] // 2
            got = moved(messages[h], lambda c: row_dim(c, h, s))
            if s > 0:
                q[h] = q[h][:half] + got[n:]
            if s < 3:
                v[h] = jnp.concatenate([v[h], got[:n]], axis=0)
            else:
                last_v[h] = got[:n]

    partial = apply_matrix(tab, matrix, v)
    send, keep = apply_matrix(tab, matrix, last_v, partial)
    w = keep + moved(send, lambda c: "c")
    g_send, g_keep = inner_product(tab, reflectors, send, keep)
    g = g_keep + moved(g_send, lambda c: "c")
    w, g = w.reshape(4, 128, 512), g.reshape(4, 64, 512)
    ch, cl, rh, rl = turned(tab, tfactor, reflectors, (v[0], last_v[0], v[1], last_v[1]))
    for s in range(2):
        w = w.reshape(-1, 2, 128, 512)
        g = g.reshape(-1, 2, 64, 512)
        n = w.shape[0]
        message = jnp.concatenate(
            [w[:, 1].reshape(n * 128, 512), g[:, 1].reshape(n * 64, 512)], axis=0
        )
        if s == 1:
            message, ch, cl, rh, rl = lax.optimization_barrier((message, ch, cl, rh, rl))
        got = moved(message, lambda c: y_dim(c, s))
        w = w[:, 0] + got[: n * 128].reshape(n, 128, 512)
        g = g[:, 0] + got[n * 128 :].reshape(n, 64, 512)
    w, g = w.reshape(128, 512), g.reshape(64, 512)

    wc = [w[:, :256], w[:, 256:]]
    last_w, last_q = [None, None], [None, None]
    w_rows = w
    for s in range(4):
        g = g + moved(g, lambda c: row_dim(c, 0, s))
        for h in range(2):
            n = wc[h].shape[0]
            got = moved(
                jnp.concatenate([wc[h], q[h]], axis=0), lambda c: row_dim(c, h, s)
            )
            if s == 0:
                q[h] = q[h] + jnp.concatenate([got[n + 32 :], got[n : n + 32]], axis=0)
            elif s < 3:
                q[h] = jnp.concatenate([q[h], got[n:]], axis=0)
            else:
                last_q[h] = got[n:]
            if s < 3:
                wc[h] = jnp.concatenate([wc[h], got[:n]], axis=0)
            else:
                last_w[h] = got[:n]
        if s < 2:
            w_rows = jnp.concatenate(
                [w_rows, moved(w_rows, lambda c: y_dim(c, s))], axis=0
            )
    w_other = moved(w_rows, lambda c: "c")
    for s in range(2):
        g = jnp.concatenate([g, moved(g, lambda c: y_dim(c, s))], axis=0)
    g_other = moved(g, lambda c: "c")

    part = update_first(tab, matrix, wc, w_rows, w_other, g, g_other, rh, rl, ch, cl)
    q_pieces = (q[0], last_q[0], q[1], last_q[1])
    return tuple(update_last(tab, part, last_w, basis_rows, q_pieces, rh, rl))


def solution(mesh):
    placed = (P("row", ("col", "grp")), P(("col", "grp"), "row"), P("row", None), P())
    return jax.shard_map(
        on_device,
        mesh=mesh,
        in_specs=placed,
        out_specs=(P("row", ("col", "grp")), P(("col", "grp"), "row")),
        check_vma=False,
    )
```

time: 187 us -> 172 us (0.920)
  local copies, waits for them, and re-layouts: 16.8 us -> 3.8 us
  starting transfers between devices: 45.6 us -> 38.6 us
  Pallas kernels: 51.8 us -> 57.6 us
    unnamed x46 -> x34, local copies, waits for them, and re-layouts: 12.6 us -> 2.36 us
    ppermute x30, starting transfers between devices: 45.6 us -> 38.6 us  [moved(): return lax.ppermute(x, EVERY, pairs)]
    pallas_call x4, Pallas kernels: 38.1 us -> 43.2 us  [the longest x1 18.2 us: update_first(): pl.pallas_call(update_first_kernel, grid_spec=pltpu.PrefetchScalarGridSpe...]
    pallas_call x1, Pallas kernels: 2.45 us -> 5.56 us  [basis_product(): pl.pallas_call(basis_kernel, grid_spec=pltpu.PrefetchScalarGridSpec(num_s...]
    pallas_call x1, Pallas kernels: 8.81 us -> 6.35 us  [turned(): pl.pallas_call(turned_kernel, grid_spec=pltpu.PrefetchScalarGridSpec(num_...]
  transfers between devices with their start and end apart: 30 -> 30, of which waited for: 18 -> 16; matrix products, arithmetic and copies ran while one was open for 6% -> 2% of each run, Pallas kernels for 7% -> 22%
where the time goes in v1:
time: 172 us; the launch traced here: 171 us
  waiting for transfers between devices  67.7 us (39%)
  Pallas kernels  57.6 us (33%)
  starting transfers between devices  38.6 us (22%)
  local copies, waits for them, and re-layouts  3.8 us (2%)
  other arithmetic  2.36 us (1%)
    ppermute x30, waiting for transfers between devices, moved(): return lax.ppermute(x, EVERY, pairs)  67.7 us
    ppermute x30, starting transfers between devices, moved(): return lax.ppermute(x, EVERY, pairs)  38.6 us
    pallas_call x1, Pallas kernels, update_first(): pl.pallas_call(update_first_kernel, grid_spec=pltpu.PrefetchScalarGridSpe...  18.2 us
    pallas_call x1, Pallas kernels, update_last(): pl.pallas_call(update_last_kernel, grid_spec=pltpu.PrefetchScalarGridSpec...  13 us
    pallas_call x2, Pallas kernels, apply_matrix(): pl.pallas_call(apply_last_kernel if last else apply_first_kernel, grid_sp...  11.9 us
    pallas_call x1, Pallas kernels, turned(): pl.pallas_call(turned_kernel, grid_spec=pltpu.PrefetchScalarGridSpec(num_...  6.35 us
    pallas_call x1, Pallas kernels, basis_product(): pl.pallas_call(basis_kernel, grid_spec=pltpu.PrefetchScalarGridSpec(num_s...  5.56 us
  transfers between devices with their start and end apart: 30, of which 16 were waited for; matrix products, arithmetic and copies ran while one was open for 2% of the time, Pallas kernels for 22%

profile of v1, /device:TPU:0, one launch (start us, length us, event | category | flops | bytes accessed | tf_op | source)
XLA Modules:
  0.0 171.4 jit_solution(3920161581009275023)
XLA Ops:
  6.1 5.6 %shard_map.68 = (f32[512,256]{1,0:T(8,128)S(1)}, f32[512,256]{1,0:T(8,128)S(1)}) custom-call(s32[64]{0:T(128)S(1)} %dynamic-slice_bitcast_fusion.tab, f32[512,1024]{1,0:T(8,128)} %b_ref.3, f32[1024,512]{1,0:T(8,128)} %v_ref.5), custom_call_target="tpu_custom_call" | custom-call | flops 1610612736 | bytes 5242880 | tf_op jit(solution)/shard_map/pallas_call | solution.py:151
  13.8 2.5 %collective-permute-start.3 = (f32[512,256]{1,0:T(8,128)S(1)}, f32[512,256]{1,0:T(8,128)S(1)}, u32[]{:S(2)}, u32[]{:S(2)}) collective-permute-start(f32[512,256]{1,0:T(8,128)S(1)} %pad_maximum_fusion.9), channel_id=1, source_target_pairs={{0,24},{1,25},{2,98},{3,99},{4,28},{5,29},{6,102},{7,103},{8,16},{... | collective-permute-start | bytes 1572872 | tf_op jit(solution)/shard_map/ppermute | solution.py:89
  16.4 4.7 %collective-permute-done.2 = f32[512,256]{1,0:T(8,128)S(1)} collective-permute-done((f32[512,256]{1,0:T(8,128)S(1)}, f32[512,256]{1,0:T(8,128)S(1)}, u32[]{:S(2)}, u32[]{:S(2)}) %collective-permute-start.2) | collective-permute-done | bytes 524320 | tf_op jit(solution)/shard_map/ppermute | solution.py:89
  21.1 3.1 %collective-permute-done.3 = f32[512,256]{1,0:T(8,128)S(1)} collective-permute-done((f32[512,256]{1,0:T(8,128)S(1)}, f32[512,256]{1,0:T(8,128)S(1)}, u32[]{:S(2)}, u32[]{:S(2)}) %collective-permute-start.3) | collective-permute-done | bytes 524320 | tf_op jit(solution)/shard_map/ppermute | solution.py:89
  26.7 9.3 %collective-permute-done.5 = f32[640,256]{1,0:T(8,128)S(1)} collective-permute-done((f32[640,256]{1,0:T(8,128)S(1)}, f32[640,256]{1,0:T(8,128)S(1)}, u32[]{:S(2)}, u32[]{:S(2)}) %collective-permute-start.5) | collective-permute-done | bytes 655392 | tf_op jit(solution)/shard_map/ppermute | solution.py:89
  38.0 2.6 %collective-permute-start.6 = (f32[1088,256]{1,0:T(8,128)S(1)}, f32[1088,256]{1,0:T(8,128)S(1)}, u32[]{:S(2)}, u32[]{:S(2)}) collective-permute-start(f32[1088,256]{1,0:T(8,128)S(1)} %constant_dynamic-update-slice_fusion), channel_id=1, source_target_pairs={{0,24},{1,25},{2,98},{3,99},{4,28},{5,29},{6,102},{7,103},{8,16},{... | collective-permute-start | bytes 3342344 | tf_op jit(solution)/shard_map/ppermute | solution.py:89
  40.9 5.8 %shard_map.69.acc = f32[1024,512]{1,0:T(8,128)S(1)} custom-call(s32[64]{0:T(128)S(1)} %dynamic-slice_bitcast_fusion.tab, f32[1024,2048]{1,0:T(8,128)S(1)} %bitcast.33, f32[1024,2048]{1,0:T(8,128)S(1)} %bitcast.33, f32[1024,2048]{1,0:T(8,128)S(1)} %bitcast.33, f32[1024,2048]{1,0:T(8,128)S(1)} %bitcast.33, f32[1024,256]{1,0:T(8,128)S(1)} %pad_maximum_fusion.p0, ...), custom_call_target="tpu_custom_call" | custom-call | flops 3221225472 | bytes 12582912 | tf_op jit(solution)/shard_map/pallas_call | solution.py:214
  46.7 8.1 %collective-permute-done.6 = f32[1088,256]{1,0:T(8,128)S(1)} collective-permute-done((f32[1088,256]{1,0:T(8,128)S(1)}, f32[1088,256]{1,0:T(8,128)S(1)}, u32[]{:S(2)}, u32[]{:S(2)}) %collective-permute-start.6) | collective-permute-done | bytes 1114144 | tf_op jit(solution)/shard_map/ppermute | solution.py:89
  56.4 6.1 %shard_map.70 = (f32[512,512]{1,0:T(8,128)S(1)}, f32[512,512]{1,0:T(8,128)S(1)}) custom-call(s32[64]{0:T(128)S(1)} %dynamic-slice_bitcast_fusion.tab, f32[1024,2048]{1,0:T(8,128)S(1)} %bitcast.33, f32[1024,2048]{1,0:T(8,128)S(1)} %bitcast.33, f32[1024,2048]{1,0:T(8,128)S(1)} %bitcast.33, f32[1024,2048]{1,0:T(8,128)S(1)} %bitcast.33, ...), custom_call_target="tpu_custom_call" | custom-call | flops 3221225472 | bytes 12582912 | tf_op jit(solution)/shard_map/pallas_call | solution.py:214
  62.8 2.5 %shard_map.71 = (f32[256,512]{1,0:T(8,128)S(1)}, f32[256,512]{1,0:T(8,128)S(1)}) custom-call(s32[64]{0:T(128)S(1)} %dynamic-slice_bitcast_fusion.tab, f32[1024,512]{1,0:T(8,128)S(1)} %copy-done, f32[512,512]{1,0:T(8,128)S(1)} %get-tuple-element.36.s_ref, f32[512,512]{1,0:T(8,128)S(1)} %get-tuple-element.35.k_ref), custom_call_target="tpu_custom_call" | custom-call | flops 1610612736 | bytes 5242880 | tf_op jit(solution)/shard_map/pallas_call | solution.py:252
  69.5 6.3 %shard_map.72 = (bf16[2048,512]{1,0:T(8,128)(2,1)S(1)}, bf16[2048,512]{1,0:T(8,128)(2,1)S(1)}, bf16[1024,512]{1,0:T(8,128)(2,1)S(1)}, bf16[1024,512]{1,0:T(8,128)(2,1)S(1)}) custom-call(s32[64]{0:T(128)S(1)} %dynamic-slice_bitcast_fusion.tab, f32[512,512]{1,0:T(8,128)S(1)} %copy-done.2, f32[1024,512]{1,0:T(8,128)S(1)} %copy-done.1, ...), custom_call_target="tpu_custom_call" | custom-call | flops 4831838208 | bytes 13631488 | tf_op jit(solution)/shard_map/pallas_call | solution.py:279
  75.9 4.1 %collective-permute-done.10 = f32[384,512]{1,0:T(8,128)S(1)} collective-permute-done((f32[384,512]{1,0:T(8,128)S(1)}, f32[384,512]{1,0:T(8,128)S(1)}, u32[]{:S(2)}, u32[]{:S(2)}) %collective-permute-start.10) | collective-permute-done | bytes 786464 | tf_op jit(solution)/shard_map/ppermute | solution.py:89
  80.2 3.1 %collective-permute-start.11 = (f32[192,512]{1,0:T(8,128)S(1)}, f32[192,512]{1,0:T(8,128)S(1)}, u32[]{:S(2)}, u32[]{:S(2)}) collective-permute-start(f32[192,512]{1,0:T(8,128)S(1)} %pad_maximum_fusion.12), channel_id=1, source_target_pairs={{0,5},{1,4},{2,6},{3,7},{4,1},{5,0},{6,2},{7,3},{8,13},{9,12},{10,... | collective-permute-start | bytes 1179656 | tf_op jit(solution)/shard_map/ppermute | solution.py:89
  84.2 5.1 %collective-permute-done.11 = f32[192,512]{1,0:T(8,128)S(1)} collective-permute-done((f32[192,512]{1,0:T(8,128)S(1)}, f32[192,512]{1,0:T(8,128)S(1)}, u32[]{:S(2)}, u32[]{:S(2)}) %collective-permute-start.11) | collective-permute-done | bytes 393248 | tf_op jit(solution)/shard_map/ppermute | solution.py:89
  94.5 4.1 %collective-permute-done.15 = f32[192,256]{1,0:T(8,128)S(1)} collective-permute-done((f32[192,256]{1,0:T(8,128)S(1)}, f32[192,256]{1,0:T(8,128)S(1)}, u32[]{:S(2)}, u32[]{:S(2)}) %collective-permute-start.15) | collective-permute-done | bytes 196640 | tf_op jit(solution)/shard_map/ppermute | solution.py:89
  101.1 4.6 %collective-permute-done.23 = f32[64,512]{1,0:T(8,128)S(1)} collective-permute-done((f32[64,512]{1,0:T(8,128)S(1)}, f32[64,512]{1,0:T(8,128)S(1)}, u32[]{:S(2)}, u32[]{:S(2)}) %collective-permute-start.23) | collective-permute-done | bytes 131104 | tf_op jit(solution)/shard_map/ppermute | solution.py:89
  105.8 2.6 %collective-permute-start.24 = (f32[64,512]{1,0:T(8,128)S(1)}, f32[64,512]{1,0:T(8,128)S(1)}, u32[]{:S(2)}, u32[]{:S(2)}) collective-permute-start(f32[64,512]{1,0:T(8,128)S(1)} %add.104), channel_id=1, source_target_pairs={{0,24},{1,25},{2,98},{3,99},{4,28},{5,29},{6,102},{7,103},{8,16},{... | collective-permute-start | bytes 393224 | tf_op jit(solution)/shard_map/ppermute | solution.py:89
  108.6 4.2 %collective-permute-start.19 = (f32[256,512]{1,0:T(8,128)S(1)}, f32[256,512]{1,0:T(8,128)S(1)}, u32[]{:S(2)}, u32[]{:S(2)}) collective-permute-start(f32[256,512]{1,0:T(8,128)S(1)} %pad_maximum_fusion.10), channel_id=1, source_target_pairs={{0,5},{1,4},{2,6},{3,7},{4,1},{5,0},{6,2},{7,3},{8,13},{9,12},{10,... | collective-permute-start | bytes 1572872 | tf_op jit(solution)/shard_map/ppermute | solution.py:89
  113.3 4.6 %collective-permute-done.13 = f32[320,256]{1,0:T(8,128)S(1)} collective-permute-done((f32[320,256]{1,0:T(8,128)S(1)}, f32[320,256]{1,0:T(8,128)S(1)}, u32[]{:S(2)}, u32[]{:S(2)}) %collective-permute-start.13) | collective-permute-done | bytes 327712 | tf_op jit(solution)/shard_map/ppermute | solution.py:89
  119.2 4.2 %collective-permute-start.26 = (f32[128,512]{1,0:T(8,128)S(1)}, f32[128,512]{1,0:T(8,128)S(1)}, u32[]{:S(2)}, u32[]{:S(2)}) collective-permute-start(f32[128,512]{1,0:T(8,128)S(1)} %pad_maximum_fusion.15), channel_id=1, source_target_pairs={{0,5},{1,4},{2,6},{3,7},{4,1},{5,0},{6,2},{7,3},{8,13},{9,12},{10,... | collective-permute-start | bytes 786440 | tf_op jit(solution)/shard_map/ppermute | solution.py:89
  124.1 3.7 %collective-permute-done.26 = f32[128,512]{1,0:T(8,128)S(1)} collective-permute-done((f32[128,512]{1,0:T(8,128)S(1)}, f32[128,512]{1,0:T(8,128)S(1)}, u32[]{:S(2)}, u32[]{:S(2)}) %collective-permute-start.26) | collective-permute-done | bytes 262176 | tf_op jit(solution)/shard_map/ppermute | solution.py:89
  129.5 8.2 %collective-permute-done.14 = f32[640,256]{1,0:T(8,128)S(1)} collective-permute-done((f32[640,256]{1,0:T(8,128)S(1)}, f32[640,256]{1,0:T(8,128)S(1)}, u32[]{:S(2)}, u32[]{:S(2)}) %collective-permute-start.14) | collective-permute-done | bytes 655392 | tf_op jit(solution)/shard_map/ppermute | solution.py:89
  139.9 18.2 %shard_map.73.a = f32[1024,2048]{1,0:T(8,128)} custom-call(s32[64]{0:T(128)S(1)} %dynamic-slice_bitcast_fusion.tab, f32[1024,2048]{1,0:T(8,128)} %a.1, f32[1024,256]{1,0:T(8,128)S(1)} %pad_maximum_fusion.2.p0, f32[1024,256]{1,0:T(8,128)S(1)} %pad_maximum_fusion.3.p1, f32[512,512]{1,0:T(8,128)S(1)} %pad_maximum_fusion.4.wk, ...), custom_call_target="tpu_custom_call" | custom-call | flops 11274289152 | bytes 27262976 | tf_op jit(solution)/shard_map/pallas_call | solution.py:359
  158.4 13.0 %shard_map.74 = (f32[1024,2048]{1,0:T(8,128)}, f32[512,1024]{1,0:T(8,128)}) custom-call(s32[64]{0:T(128)S(1)} %dynamic-slice_bitcast_fusion.tab, f32[1024,2048]{1,0:T(8,128)} %shard_map.73.a, f32[1024,256]{1,0:T(8,128)S(1)} %slice.279.p0, f32[1024,256]{1,0:T(8,128)S(1)} %slice.281.p1, bf16[1024,512]{1,0:T(8,128)(2,1)S(1)} %get-tuple-element.44.rh.xh, ...), custom_call_target="tpu_custom_call" | custom-call | flops 4831838208 | bytes 27262976 | tf_op jit(solution)/shard_map/pallas_call | solution.py:384
  (142 shorter events, 33.6 us)
Async XLA Ops:
  1.7 10.1 %collective-permute-start = (f32[128,256]{1,0:T(8,128)S(1)}, f32[128,256]{1,0:T(8,128)S(1)}, u32[]{:S(2)}, u32[]{:S(2)}) collective-permute-start(f32[128,256]{1,0:T(8,128)S(1)} %get-tuple-element.25), channel_id=1, source_target_pairs={{0,32},{1,33},{2,10},{3,11},{4,36},{5,37},{6,14},{7,15},{8,40},{9,... | collective-permute-start | bytes 393224 | tf_op jit(solution)/shard_map/ppermute | solution.py:89
  3.3 8.4 %collective-permute-start.1 = (f32[128,256]{1,0:T(8,128)S(1)}, f32[128,256]{1,0:T(8,128)S(1)}, u32[]{:S(2)}, u32[]{:S(2)}) collective-permute-start(f32[128,256]{1,0:T(8,128)S(1)} %get-tuple-element.27), channel_id=1, source_target_pairs={{0,96},{1,97},{2,26},{3,27},{4,100},{5,101},{6,30},{7,31},{8,104},... | collective-permute-start | bytes 393224 | tf_op jit(solution)/shard_map/ppermute | solution.py:89
  11.8 9.3 %collective-permute-start.2 = (f32[512,256]{1,0:T(8,128)S(1)}, f32[512,256]{1,0:T(8,128)S(1)}, u32[]{:S(2)}, u32[]{:S(2)}) collective-permute-start(f32[512,256]{1,0:T(8,128)S(1)} %pad_maximum_fusion.8), channel_id=1, source_target_pairs={{0,8},{1,9},{2,34},{3,35},{4,12},{5,13},{6,38},{7,39},{8,0},{9,1},... | collective-permute-start | bytes 1572872 | tf_op jit(solution)/shard_map/ppermute | solution.py:89
  13.8 10.4 %collective-permute-start.3 = (f32[512,256]{1,0:T(8,128)S(1)}, f32[512,256]{1,0:T(8,128)S(1)}, u32[]{:S(2)}, u32[]{:S(2)}) collective-permute-start(f32[512,256]{1,0:T(8,128)S(1)} %pad_maximum_fusion.9), channel_id=1, source_target_pairs={{0,24},{1,25},{2,98},{3,99},{4,28},{5,29},{6,102},{7,103},{8,16},{... | collective-permute-start | bytes 1572872 | tf_op jit(solution)/shard_map/ppermute | solution.py:89
  25.4 10.7 %collective-permute-start.5 = (f32[640,256]{1,0:T(8,128)S(1)}, f32[640,256]{1,0:T(8,128)S(1)}, u32[]{:S(2)}, u32[]{:S(2)}) collective-permute-start(f32[640,256]{1,0:T(8,128)S(1)} %pad_maximum_fusion.7), channel_id=1, source_target_pairs={{0,32},{1,33},{2,10},{3,11},{4,36},{5,37},{6,14},{7,15},{8,40},{9,... | collective-permute-start | bytes 1966088 | tf_op jit(solution)/shard_map/ppermute | solution.py:89
  26.1 11.8 %collective-permute-start.4 = (f32[640,256]{1,0:T(8,128)S(1)}, f32[640,256]{1,0:T(8,128)S(1)}, u32[]{:S(2)}, u32[]{:S(2)}) collective-permute-start(f32[640,256]{1,0:T(8,128)S(1)} %pad_maximum_fusion.6), channel_id=1, source_target_pairs={{0,96},{1,97},{2,26},{3,27},{4,100},{5,101},{6,30},{7,31},{8,104},... | collective-permute-start | bytes 1966088 | tf_op jit(solution)/shard_map/ppermute | solution.py:89
  38.0 16.8 %collective-permute-start.6 = (f32[1088,256]{1,0:T(8,128)S(1)}, f32[1088,256]{1,0:T(8,128)S(1)}, u32[]{:S(2)}, u32[]{:S(2)}) collective-permute-start(f32[1088,256]{1,0:T(8,128)S(1)} %constant_dynamic-update-slice_fusion), channel_id=1, source_target_pairs={{0,24},{1,25},{2,98},{3,99},{4,28},{5,29},{6,102},{7,103},{8,16},{... | collective-permute-start | bytes 3342344 | tf_op jit(solution)/shard_map/ppermute | solution.py:89
  40.6 15.7 %collective-permute-start.7 = (f32[1088,256]{1,0:T(8,128)}, f32[1088,256]{1,0:T(8,128)S(1)}, u32[]{:S(2)}, u32[]{:S(2)}) collective-permute-start(f32[1088,256]{1,0:T(8,128)} %copy-done.4), channel_id=1, source_target_pairs={{0,8},{1,9},{2,34},{3,35},{4,12},{5,13},{6,38},{7,39},{8,0},{9,1},... | collective-permute-start | bytes 3342344 | tf_op jit(solution)/shard_map/ppermute | solution.py:89
  67.9 12.1 %collective-permute-start.10 = (f32[384,512]{1,0:T(8,128)S(1)}, f32[384,512]{1,0:T(8,128)S(1)}, u32[]{:S(2)}, u32[]{:S(2)}) collective-permute-start(f32[384,512]{1,0:T(8,128)S(1)} %pad_maximum_fusion.5), channel_id=1, source_target_pairs={{0,4},{1,5},{2,7},{3,6},{4,0},{5,1},{6,3},{7,2},{8,12},{9,13},{10,... | collective-permute-start | bytes 2359304 | tf_op jit(solution)/shard_map/ppermute | solution.py:89
  80.2 9.1 %collective-permute-start.11 = (f32[192,512]{1,0:T(8,128)S(1)}, f32[192,512]{1,0:T(8,128)S(1)}, u32[]{:S(2)}, u32[]{:S(2)}) collective-permute-start(f32[192,512]{1,0:T(8,128)S(1)} %pad_maximum_fusion.12), channel_id=1, source_target_pairs={{0,5},{1,4},{2,6},{3,7},{4,1},{5,0},{6,2},{7,3},{8,13},{9,12},{10,... | collective-permute-start | bytes 1179656 | tf_op jit(solution)/shard_map/ppermute | solution.py:89
  91.4 7.2 %collective-permute-start.15 = (f32[192,256]{1,0:T(8,128)S(1)}, f32[192,256]{1,0:T(8,128)S(1)}, u32[]{:S(2)}, u32[]{:S(2)}) collective-permute-start(f32[192,256]{1,0:T(8,128)S(1)} %pad_maximum_fusion.19), channel_id=1, source_target_pairs={{0,96},{1,97},{2,26},{3,27},{4,100},{5,101},{6,30},{7,31},{8,104},... | collective-permute-start | bytes 589832 | tf_op jit(solution)/shard_map/ppermute | solution.py:89
  91.6 16.9 %collective-permute-start.18 = (f32[128,512]{1,0:T(8,128)S(1)}, f32[128,512]{1,0:T(8,128)S(1)}, u32[]{:S(2)}, u32[]{:S(2)}) collective-permute-start(f32[128,512]{1,0:T(8,128)S(1)} %slice_add_fusion), channel_id=1, source_target_pairs={{0,4},{1,5},{2,7},{3,6},{4,0},{5,1},{6,3},{7,2},{8,12},{9,13},{10,... | collective-permute-start | bytes 786440 | tf_op jit(solution)/shard_map/ppermute | solution.py:89
  92.1 7.3 %collective-permute-start.12 = (f32[192,256]{1,0:T(8,128)S(1)}, f32[192,256]{1,0:T(8,128)S(1)}, u32[]{:S(2)}, u32[]{:S(2)}) collective-permute-start(f32[192,256]{1,0:T(8,128)S(1)} %pad_maximum_fusion.18), channel_id=1, source_target_pairs={{0,32},{1,33},{2,10},{3,11},{4,36},{5,37},{6,14},{7,15},{8,40},{9,... | collective-permute-start | bytes 589832 | tf_op jit(solution)/shard_map/ppermute | solution.py:89
  98.6 14.3 %collective-permute-start.16 = (f32[320,256]{1,0:T(8,128)S(1)}, f32[320,256]{1,0:T(8,128)S(1)}, u32[]{:S(2)}, u32[]{:S(2)}) collective-permute-start(f32[320,256]{1,0:T(8,128)S(1)} %pad_maximum_fusion.14), channel_id=1, source_target_pairs={{0,24},{1,25},{2,98},{3,99},{4,28},{5,29},{6,102},{7,103},{8,16},{... | collective-permute-start | bytes 983048 | tf_op jit(solution)/shard_map/ppermute | solution.py:89
  105.8 7.0 %collective-permute-start.24 = (f32[64,512]{1,0:T(8,128)S(1)}, f32[64,512]{1,0:T(8,128)S(1)}, u32[]{:S(2)}, u32[]{:S(2)}) collective-permute-start(f32[64,512]{1,0:T(8,128)S(1)} %add.104), channel_id=1, source_target_pairs={{0,24},{1,25},{2,98},{3,99},{4,28},{5,29},{6,102},{7,103},{8,16},{... | collective-permute-start | bytes 393224 | tf_op jit(solution)/shard_map/ppermute | solution.py:89
  108.4 9.5 %collective-permute-start.13 = (f32[320,256]{1,0:T(8,128)S(1)}, f32[320,256]{1,0:T(8,128)S(1)}, u32[]{:S(2)}, u32[]{:S(2)}) collective-permute-start(f32[320,256]{1,0:T(8,128)S(1)} %pad_maximum_fusion.13), channel_id=1, source_target_pairs={{0,8},{1,9},{2,34},{3,35},{4,12},{5,13},{6,38},{7,39},{8,0},{9,1},... | collective-permute-start | bytes 983048 | tf_op jit(solution)/shard_map/ppermute | solution.py:89
  108.6 15.4 %collective-permute-start.19 = (f32[256,512]{1,0:T(8,128)S(1)}, f32[256,512]{1,0:T(8,128)S(1)}, u32[]{:S(2)}, u32[]{:S(2)}) collective-permute-start(f32[256,512]{1,0:T(8,128)S(1)} %pad_maximum_fusion.10), channel_id=1, source_target_pairs={{0,5},{1,4},{2,6},{3,7},{4,1},{5,0},{6,2},{7,3},{8,13},{9,12},{10,... | collective-permute-start | bytes 1572872 | tf_op jit(solution)/shard_map/ppermute | solution.py:89
  113.0 14.9 %collective-permute-start.17 = (f32[640,256]{1,0:T(8,128)S(1)}, f32[640,256]{1,0:T(8,128)S(1)}, u32[]{:S(2)}, u32[]{:S(2)}) collective-permute-start(f32[640,256]{1,0:T(8,128)S(1)} %get-tuple-element.73), channel_id=1, source_target_pairs={{0,32},{1,33},{2,10},{3,11},{4,36},{5,37},{6,14},{7,15},{8,40},{9,... | collective-permute-start | bytes 1966088 | tf_op jit(solution)/shard_map/ppermute | solution.py:89
  119.2 8.5 %collective-permute-start.26 = (f32[128,512]{1,0:T(8,128)S(1)}, f32[128,512]{1,0:T(8,128)S(1)}, u32[]{:S(2)}, u32[]{:S(2)}) collective-permute-start(f32[128,512]{1,0:T(8,128)S(1)} %pad_maximum_fusion.15), channel_id=1, source_target_pairs={{0,5},{1,4},{2,6},{3,7},{4,1},{5,0},{6,2},{7,3},{8,13},{9,12},{10,... | collective-permute-start | bytes 786440 | tf_op jit(solution)/shard_map/ppermute | solution.py:89
  123.4 14.2 %collective-permute-start.14 = (f32[640,256]{1,0:T(8,128)S(1)}, f32[640,256]{1,0:T(8,128)S(1)}, u32[]{:S(2)}, u32[]{:S(2)}) collective-permute-start(f32[640,256]{1,0:T(8,128)S(1)} %get-tuple-element.75), channel_id=1, source_target_pairs={{0,96},{1,97},{2,26},{3,27},{4,100},{5,101},{6,30},{7,31},{8,104},... | collective-permute-start | bytes 1966088 | tf_op jit(solution)/shard_map/ppermute | solution.py:89
  124.0 15.9 %collective-permute-start.20 = (f32[512,512]{1,0:T(8,128)S(1)}, f32[512,512]{1,0:T(8,128)S(1)}, u32[]{:S(2)}, u32[]{:S(2)}) collective-permute-start(f32[512,512]{1,0:T(8,128)S(1)} %pad_maximum_fusion.4.wk), channel_id=1, source_target_pairs={{0,2},{1,3},{2,0},{3,1},{4,6},{5,7},{6,4},{7,5},{8,10},{9,11},{10,... | collective-permute-start | bytes 3145736 | tf_op jit(solution)/shard_map/ppermute | solution.py:89
  127.8 12.1 %collective-permute-start.27 = (f32[256,512]{1,0:T(8,128)S(1)}, f32[256,512]{1,0:T(8,128)S(1)}, u32[]{:S(2)}, u32[]{:S(2)}) collective-permute-start(f32[256,512]{1,0:T(8,128)S(1)} %pad_maximum_fusion.11.gk), channel_id=1, source_target_pairs={{0,2},{1,3},{2,0},{3,1},{4,6},{5,7},{6,4},{7,5},{8,10},{9,11},{10,... | collective-permute-start | bytes 1572872 | tf_op jit(solution)/shard_map/ppermute | solution.py:89
  128.1 30.1 %collective-permute-start.29 = (f32[1280,256]{1,0:T(8,128)S(1)}, f32[1280,256]{1,0:T(8,128)S(1)}, u32[]{:S(2)}, u32[]{:S(2)}) collective-permute-start(f32[1280,256]{1,0:T(8,128)S(1)} %get-tuple-element.55), channel_id=1, source_target_pairs={{0,8},{1,9},{2,34},{3,35},{4,12},{5,13},{6,38},{7,39},{8,0},{9,1},... | collective-permute-start | bytes 3932168 | tf_op jit(solution)/shard_map/ppermute | solution.py:89
  137.8 20.5 %collective-permute-start.28 = (f32[1280,256]{1,0:T(8,128)S(1)}, f32[1280,256]{1,0:T(8,128)S(1)}, u32[]{:S(2)}, u32[]{:S(2)}) collective-permute-start(f32[1280,256]{1,0:T(8,128)S(1)} %get-tuple-element.57), channel_id=1, source_target_pairs={{0,24},{1,25},{2,98},{3,99},{4,28},{5,29},{6,102},{7,103},{8,16},{... | collective-permute-start | bytes 3932168 | tf_op jit(solution)/shard_map/ppermute | solution.py:89
  (15 other events, 90.9 us)

commit v2 on v1

--- a/solution.py
+++ b/solution.py
@@ -128,23 +128,13 @@
     return pl.BlockSpec(shape, lambda s, t: (s, 0))
 
 
-def basis_kernel(tab, b_ref, v_ref, q0_ref, q1_ref, q, vh, vl):
-    step = pl.program_id(0)
-
-    @pl.when(step == 0)
-    def _():
-        vh[...], vl[...] = split(v_ref[...])
-
-    rows = pl.ds(pl.multiple_of(step * 128, 128), 128)
-    q[rows, :] = dot3(split(b_ref[...]), (vh[...], vl[...]), NN)
-
-    @pl.when(step == 3)
-    def _():
-        for h, out in enumerate((q0_ref, q1_ref)):
-            for j in range(16):
-                place = (j >> 1 & 1) * 8 + (j >> 2 & 1) * 4 + (j >> 3 & 1) * 2 + (j & 1)
-                rows = pl.ds(pl.multiple_of(tab[h * 16 + j] * 32, 32), 32)
-                out[place * 32 : place * 32 + 32, :] = q[rows, h * 256 : h * 256 + 256]
+def basis_kernel(tab, b_ref, v_ref, q0_ref, q1_ref, q):
+    q[...] = dot3(split(b_ref[...]), split(v_ref[...]), NN)
+    for h, out in enumerate((q0_ref, q1_ref)):
+        for j in range(16):
+            place = (j >> 1 & 1) * 8 + (j >> 2 & 1) * 4 + (j >> 3 & 1) * 2 + (j & 1)
+            rows = pl.ds(pl.multiple_of(tab[h * 16 + j] * 32, 32), 32)
+            out[place * 32 : place * 32 + 32, :] = q[rows, h * 256 : h * 256 + 256]
 
 
 def basis_product(tab, basis, v):
@@ -152,14 +142,13 @@
         basis_kernel,
         grid_spec=pltpu.PrefetchScalarGridSpec(
             num_scalar_prefetch=1,
-            grid=(4,),
-            in_specs=[tiled((128, 1024)), full((1024, 512))],
+            grid=(1,),
+            in_specs=[full((512, 1024)), full((1024, 512))],
             out_specs=[full((512, 256))] * 2,
-            scratch_shapes=[pltpu.VMEM((512, 512), F32)]
-            + [pltpu.VMEM((1024, 512), BF16)] * 2,
+            scratch_shapes=[pltpu.VMEM((512, 512), F32)],
         ),
         out_shape=[jax.ShapeDtypeStruct((512, 256), F32)] * 2,
-        compiler_params=params(16),
+        compiler_params=params(32),
         cost_estimate=cost(512 * 1024 * 512, 5 << 20),
     )(tab, in_hbm(basis), in_hbm(v))
 
@@ -300,21 +289,26 @@
         b3[h, :, 512:] = bh
 
 
-def less_blocks(tab, first, out, x, b3):
+def less_blocks(tab, first, src, src_rows, out, rows, x, b3, part):
     for h in range(2):
         cols = slice(h * 256, h * 256 + 256)
         left = jnp.concatenate([x[0][:, cols], x[0][:, cols], x[1][:, cols]], axis=1)
-        for p in range(4):
-            right = b3[h, p * 256 : p * 256 + 256, :]
-            part = lax.dot_general(left, right, NT, preferred_element_type=F32)
-            for e in range(2):
-                at = tab[h * 16 + first + p * 2 + e] * 128
+        part[h] = lax.dot_general(left, b3[h], NT, preferred_element_type=F32)
+    for h in range(2):
+        for j in range(8):
+            at = tab[h * 16 + first + j] * 128
+            at = pl.ds(pl.multiple_of(at, 128), 128)
+            old = src[src_rows, at] if h == 0 else out[rows, at]
+            out[rows, at] = old - part[h, :, j * 128 : j * 128 + 128]
+        if h == 0 and src is not out:
+            for j in range(8):
+                at = tab[(first + j + 8) % 16] * 128
                 at = pl.ds(pl.multiple_of(at, 128), 128)
-                out[:, at] = out[:, at] - part[:, e * 128 : e * 128 + 128]
+                out[rows, at] = src[src_rows, at]
 
 
 def update_first_kernel(
-    tab, a, p0, p1, wk, ws, gk, gs, rh, rl, ch, cl, out, b3, w, g, gh, gl
+    tab, a, p0, p1, wk, ws, gk, gs, rh, rl, ch, cl, out, b3, part, w, g, gh, gl
 ):
     step = pl.program_id(0)
 
@@ -334,13 +328,13 @@
     left = split(w[rows, :] - dot3(x, (gh[...], gl[...]), NN))
     for i in range(4):
         at = slice(i * 512, i * 512 + 512)
-        out[:, at] = a[:, at] - dot3(left, (ch[at, :], cl[at, :]), NT)
-    less_blocks(tab, 0, out, x, b3)
+        out[rows, at] = a[:, at] - dot3(left, (ch[at, :], cl[at, :]), NT)
+    less_blocks(tab, 0, out, rows, out, rows, x, b3, part)
 
 
 def update_last_kernel(
     tab, a, p0, p1, rh, rl, b_ref, q0, q1, q2, q3, xh, xl, out, b_out,
-    b3, qh, ql,
+    b3, part, qh, ql,
 ):
     step = pl.program_id(0)
 
@@ -349,8 +343,9 @@
         place_cat((p0, p1), b3)
         place_blocks(tab, (q0, q1, q2, q3), qh, ql, 32)
 
-    out[...] = a[...]
-    less_blocks(tab, 8, out, (rh[...], rl[...]), b3)
+    acc_rows = pl.ds(pl.multiple_of(step * 256, 256), 256)
+    x = (rh[...], rl[...])
+    less_blocks(tab, 8, a, acc_rows, out, slice(None), x, b3, part)
     rows = pl.ds(pl.multiple_of(step * 128, 128), 128)
     b_out[...] = b_ref[...] - dot3((qh[rows, :], ql[rows, :]), (xh[...], xl[...]), NT)
 
@@ -365,13 +360,13 @@
             + [WHOLE] * 6
             + [tiled((256, 512))] * 2
             + [WHOLE] * 2,
-            out_specs=tiled((256, 2048)),
-            scratch_shapes=[pltpu.VMEM((2, 1024, 768), BF16)]
+            out_specs=WHOLE,
+            scratch_shapes=[pltpu.VMEM((2, 1024, 768), BF16), pltpu.VMEM((2, 256, 1024), F32)]
             + [pltpu.VMEM((1024, 512), F32), pltpu.VMEM((512, 512), F32)]
             + [pltpu.VMEM((512, 512), BF16)] * 2,
         ),
-        out_shape=pltpu.HBM((1024, 2048), F32),
-        compiler_params=params(26),
+        out_shape=pltpu.VMEM((1024, 2048), F32),
+        compiler_params=params(24),
         cost_estimate=cost(7 * 1024 * 512 * 512, 26 << 20),
     )(
         tab, in_hbm(matrix),
@@ -386,23 +381,25 @@
         grid_spec=pltpu.PrefetchScalarGridSpec(
             num_scalar_prefetch=1,
             grid=(4,),
-            in_specs=[tiled((256, 2048))]
-            + [full((1024, 256))] * 2
+            in_specs=[WHOLE] * 3
             + [tiled((256, 512))] * 2
             + [tiled((128, 1024))]
-            + [full((256, 256))] * 4
-            + [full((1024, 512))] * 2,
+            + [WHOLE] * 6,
             out_specs=[tiled((256, 2048)), tiled((128, 1024))],
-            scratch_shapes=[pltpu.VMEM((2, 1024, 768), BF16)]
+            scratch_shapes=[pltpu.VMEM((2, 1024, 768), BF16), pltpu.VMEM((2, 256, 1024), F32)]
             + [pltpu.VMEM((512, 512), BF16)] * 2,
         ),
         out_shape=[
             jax.ShapeDtypeStruct((1024, 2048), F32),
             jax.ShapeDtypeStruct((512, 1024), F32),
         ],
-        compiler_params=params(28),
+        compiler_params=params(20),
         cost_estimate=cost(3 * 1024 * 512 * 512, 26 << 20),
-    )(tab, in_hbm(acc), *pieces, rh, rl, in_hbm(basis), *q_pieces, rh, rl)
+    )(
+        tab, *[in_vmem(x) for x in (acc, *pieces)],
+        rh, rl, in_hbm(basis),
+        *[in_vmem(x) for x in (*q_pieces, rh, rl)],
+    )
 
 
 def on_device(matrix, basis_rows, reflectors, tfactor):

time: 172 us -> 169 us (0.983)
  Pallas kernels: 57.6 us -> 55.2 us
  transfers between devices with their start and end apart: 30 -> 30, of which waited for: 16 -> 16; matrix products, arithmetic and copies ran while one was open for 2% -> 2% of each run, Pallas kernels for 22% -> 21%
where the time goes in v2:
time: 169 us
  waiting for transfers between devices  67.8 us (40%)
  Pallas kernels  55.2 us (33%)
  starting transfers between devices  38.5 us (23%)
  local copies, waits for them, and re-layouts  3.75 us (2%)
  other arithmetic  2.39 us (1%)
    ppermute x30, waiting for transfers between devices, moved(): return lax.ppermute(x, EVERY, pairs)  67.8 us
    ppermute x30, starting transfers between devices, moved(): return lax.ppermute(x, EVERY, pairs)  38.5 us
    pallas_call x1, Pallas kernels, update_first(): pl.pallas_call(update_first_kernel, grid_spec=pltpu.PrefetchScalarGridSpe...  16.9 us
    pallas_call x1, Pallas kernels, update_last(): pl.pallas_call(update_last_kernel, grid_spec=pltpu.PrefetchScalarGridSpec...  12.9 us
    pallas_call x2, Pallas kernels, apply_matrix(): pl.pallas_call(apply_last_kernel if last else apply_first_kernel, grid_sp...  11.9 us
    pallas_call x1, Pallas kernels, turned(): pl.pallas_call(turned_kernel, grid_spec=pltpu.PrefetchScalarGridSpec(num_...  6.34 us
    pallas_call x1, Pallas kernels, basis_product(): pl.pallas_call(basis_kernel, grid_spec=pltpu.PrefetchScalarGridSpec(num_s...  4.62 us
  transfers between devices with their start and end apart: 30, of which 16 were waited for; matrix products, arithmetic and copies ran while one was open for 2% of the time, Pallas kernels for 21%

profile of v2, /device:TPU:0, one launch (start us, length us, event | category | flops | bytes accessed | tf_op | source)
XLA Modules:
  0.0 169.0 jit_solution(7504443900673372976)
XLA Ops:
  6.1 4.6 %shard_map.68 = (f32[512,256]{1,0:T(8,128)S(1)}, f32[512,256]{1,0:T(8,128)S(1)}) custom-call(s32[64]{0:T(128)S(1)} %dynamic-slice_bitcast_fusion.tab, f32[512,1024]{1,0:T(8,128)} %b_ref.3, f32[1024,512]{1,0:T(8,128)} %v_ref.5), custom_call_target="tpu_custom_call" | custom-call | flops 1610612736 | bytes 5242880 | tf_op jit(solution)/shard_map/pallas_call | solution.py:141
  12.9 2.5 %collective-permute-start.3 = (f32[512,256]{1,0:T(8,128)S(1)}, f32[512,256]{1,0:T(8,128)S(1)}, u32[]{:S(2)}, u32[]{:S(2)}) collective-permute-start(f32[512,256]{1,0:T(8,128)S(1)} %pad_maximum_fusion.9), channel_id=1, source_target_pairs={{0,24},{1,25},{2,98},{3,99},{4,28},{5,29},{6,102},{7,103},{8,16},{... | collective-permute-start | bytes 1572872 | tf_op jit(solution)/shard_map/ppermute | solution.py:89
  15.4 4.7 %collective-permute-done.2 = f32[512,256]{1,0:T(8,128)S(1)} collective-permute-done((f32[512,256]{1,0:T(8,128)S(1)}, f32[512,256]{1,0:T(8,128)S(1)}, u32[]{:S(2)}, u32[]{:S(2)}) %collective-permute-start.2) | collective-permute-done | bytes 524320 | tf_op jit(solution)/shard_map/ppermute | solution.py:89
  20.1 3.1 %collective-permute-done.3 = f32[512,256]{1,0:T(8,128)S(1)} collective-permute-done((f32[512,256]{1,0:T(8,128)S(1)}, f32[512,256]{1,0:T(8,128)S(1)}, u32[]{:S(2)}, u32[]{:S(2)}) %collective-permute-start.3) | collective-permute-done | bytes 524320 | tf_op jit(solution)/shard_map/ppermute | solution.py:89
  25.6 9.4 %collective-permute-done.5 = f32[640,256]{1,0:T(8,128)S(1)} collective-permute-done((f32[640,256]{1,0:T(8,128)S(1)}, f32[640,256]{1,0:T(8,128)S(1)}, u32[]{:S(2)}, u32[]{:S(2)}) %collective-permute-start.5) | collective-permute-done | bytes 655392 | tf_op jit(solution)/shard_map/ppermute | solution.py:89
  36.9 2.6 %collective-permute-start.6 = (f32[1088,256]{1,0:T(8,128)S(1)}, f32[1088,256]{1,0:T(8,128)S(1)}, u32[]{:S(2)}, u32[]{:S(2)}) collective-permute-start(f32[1088,256]{1,0:T(8,128)S(1)} %constant_dynamic-update-slice_fusion), channel_id=1, source_target_pairs={{0,24},{1,25},{2,98},{3,99},{4,28},{5,29},{6,102},{7,103},{8,16},{... | collective-permute-start | bytes 3342344 | tf_op jit(solution)/shard_map/ppermute | solution.py:89
  39.8 5.8 %shard_map.69.acc = f32[1024,512]{1,0:T(8,128)S(1)} custom-call(s32[64]{0:T(128)S(1)} %dynamic-slice_bitcast_fusion.tab, f32[1024,2048]{1,0:T(8,128)S(1)} %bitcast.33, f32[1024,2048]{1,0:T(8,128)S(1)} %bitcast.33, f32[1024,2048]{1,0:T(8,128)S(1)} %bitcast.33, f32[1024,2048]{1,0:T(8,128)S(1)} %bitcast.33, f32[1024,256]{1,0:T(8,128)S(1)} %pad_maximum_fusion.p0, ...), custom_call_target="tpu_custom_call" | custom-call | flops 3221225472 | bytes 12582912 | tf_op jit(solution)/shard_map/pallas_call | solution.py:203
  45.7 8.1 %collective-permute-done.6 = f32[1088,256]{1,0:T(8,128)S(1)} collective-permute-done((f32[1088,256]{1,0:T(8,128)S(1)}, f32[1088,256]{1,0:T(8,128)S(1)}, u32[]{:S(2)}, u32[]{:S(2)}) %collective-permute-start.6) | collective-permute-done | bytes 1114144 | tf_op jit(solution)/shard_map/ppermute | solution.py:89
  55.3 6.1 %shard_map.70 = (f32[512,512]{1,0:T(8,128)S(1)}, f32[512,512]{1,0:T(8,128)S(1)}) custom-call(s32[64]{0:T(128)S(1)} %dynamic-slice_bitcast_fusion.tab, f32[1024,2048]{1,0:T(8,128)S(1)} %bitcast.33, f32[1024,2048]{1,0:T(8,128)S(1)} %bitcast.33, f32[1024,2048]{1,0:T(8,128)S(1)} %bitcast.33, f32[1024,2048]{1,0:T(8,128)S(1)} %bitcast.33, ...), custom_call_target="tpu_custom_call" | custom-call | flops 3221225472 | bytes 12582912 | tf_op jit(solution)/shard_map/pallas_call | solution.py:203
  61.8 2.5 %shard_map.71 = (f32[256,512]{1,0:T(8,128)S(1)}, f32[256,512]{1,0:T(8,128)S(1)}) custom-call(s32[64]{0:T(128)S(1)} %dynamic-slice_bitcast_fusion.tab, f32[1024,512]{1,0:T(8,128)S(1)} %copy-done, f32[512,512]{1,0:T(8,128)S(1)} %get-tuple-element.36.s_ref, f32[512,512]{1,0:T(8,128)S(1)} %get-tuple-element.35.k_ref), custom_call_target="tpu_custom_call" | custom-call | flops 1610612736 | bytes 5242880 | tf_op jit(solution)/shard_map/pallas_call | solution.py:241
  68.5 6.3 %shard_map.72 = (bf16[2048,512]{1,0:T(8,128)(2,1)S(1)}, bf16[2048,512]{1,0:T(8,128)(2,1)S(1)}, bf16[1024,512]{1,0:T(8,128)(2,1)S(1)}, bf16[1024,512]{1,0:T(8,128)(2,1)S(1)}) custom-call(s32[64]{0:T(128)S(1)} %dynamic-slice_bitcast_fusion.tab, f32[512,512]{1,0:T(8,128)S(1)} %copy-done.2, f32[1024,512]{1,0:T(8,128)S(1)} %copy-done.1, ...), custom_call_target="tpu_custom_call" | custom-call | flops 4831838208 | bytes 13631488 | tf_op jit(solution)/shard_map/pallas_call | solution.py:268
  74.8 4.1 %collective-permute-done.10 = f32[384,512]{1,0:T(8,128)S(1)} collective-permute-done((f32[384,512]{1,0:T(8,128)S(1)}, f32[384,512]{1,0:T(8,128)S(1)}, u32[]{:S(2)}, u32[]{:S(2)}) %collective-permute-start.10) | collective-permute-done | bytes 786464 | tf_op jit(solution)/shard_map/ppermute | solution.py:89
  79.2 3.1 %collective-permute-start.11 = (f32[192,512]{1,0:T(8,128)S(1)}, f32[192,512]{1,0:T(8,128)S(1)}, u32[]{:S(2)}, u32[]{:S(2)}) collective-permute-start(f32[192,512]{1,0:T(8,128)S(1)} %pad_maximum_fusion.12), channel_id=1, source_target_pairs={{0,5},{1,4},{2,6},{3,7},{4,1},{5,0},{6,2},{7,3},{8,13},{9,12},{10,... | collective-permute-start | bytes 1179656 | tf_op jit(solution)/shard_map/ppermute | solution.py:89
  83.1 5.1 %collective-permute-done.11 = f32[192,512]{1,0:T(8,128)S(1)} collective-permute-done((f32[192,512]{1,0:T(8,128)S(1)}, f32[192,512]{1,0:T(8,128)S(1)}, u32[]{:S(2)}, u32[]{:S(2)}) %collective-permute-start.11) | collective-permute-done | bytes 393248 | tf_op jit(solution)/shard_map/ppermute | solution.py:89
  93.4 4.1 %collective-permute-done.15 = f32[192,256]{1,0:T(8,128)S(1)} collective-permute-done((f32[192,256]{1,0:T(8,128)S(1)}, f32[192,256]{1,0:T(8,128)S(1)}, u32[]{:S(2)}, u32[]{:S(2)}) %collective-permute-start.15) | collective-permute-done | bytes 196640 | tf_op jit(solution)/shard_map/ppermute | solution.py:89
  100.1 4.6 %collective-permute-done.23 = f32[64,512]{1,0:T(8,128)S(1)} collective-permute-done((f32[64,512]{1,0:T(8,128)S(1)}, f32[64,512]{1,0:T(8,128)S(1)}, u32[]{:S(2)}, u32[]{:S(2)}) %collective-permute-start.23) | collective-permute-done | bytes 131104 | tf_op jit(solution)/shard_map/ppermute | solution.py:89
  104.7 2.7 %collective-permute-start.24 = (f32[64,512]{1,0:T(8,128)S(1)}, f32[64,512]{1,0:T(8,128)S(1)}, u32[]{:S(2)}, u32[]{:S(2)}) collective-permute-start(f32[64,512]{1,0:T(8,128)S(1)} %add.104), channel_id=1, source_target_pairs={{0,24},{1,25},{2,98},{3,99},{4,28},{5,29},{6,102},{7,103},{8,16},{... | collective-permute-start | bytes 393224 | tf_op jit(solution)/shard_map/ppermute | solution.py:89
  107.6 4.1 %collective-permute-start.19 = (f32[256,512]{1,0:T(8,128)S(1)}, f32[256,512]{1,0:T(8,128)S(1)}, u32[]{:S(2)}, u32[]{:S(2)}) collective-permute-start(f32[256,512]{1,0:T(8,128)S(1)} %pad_maximum_fusion.10), channel_id=1, source_target_pairs={{0,5},{1,4},{2,6},{3,7},{4,1},{5,0},{6,2},{7,3},{8,13},{9,12},{10,... | collective-permute-start | bytes 1572872 | tf_op jit(solution)/shard_map/ppermute | solution.py:89
  112.3 4.7 %collective-permute-done.13 = f32[320,256]{1,0:T(8,128)S(1)} collective-permute-done((f32[320,256]{1,0:T(8,128)S(1)}, f32[320,256]{1,0:T(8,128)S(1)}, u32[]{:S(2)}, u32[]{:S(2)}) %collective-permute-start.13) | collective-permute-done | bytes 327712 | tf_op jit(solution)/shard_map/ppermute | solution.py:89
  118.2 4.2 %collective-permute-start.26 = (f32[128,512]{1,0:T(8,128)S(1)}, f32[128,512]{1,0:T(8,128)S(1)}, u32[]{:S(2)}, u32[]{:S(2)}) collective-permute-start(f32[128,512]{1,0:T(8,128)S(1)} %pad_maximum_fusion.15), channel_id=1, source_target_pairs={{0,5},{1,4},{2,6},{3,7},{4,1},{5,0},{6,2},{7,3},{8,13},{9,12},{10,... | collective-permute-start | bytes 786440 | tf_op jit(solution)/shard_map/ppermute | solution.py:89
  123.1 3.7 %collective-permute-done.26 = f32[128,512]{1,0:T(8,128)S(1)} collective-permute-done((f32[128,512]{1,0:T(8,128)S(1)}, f32[128,512]{1,0:T(8,128)S(1)}, u32[]{:S(2)}, u32[]{:S(2)}) %collective-permute-start.26) | collective-permute-done | bytes 262176 | tf_op jit(solution)/shard_map/ppermute | solution.py:89
  128.5 8.2 %collective-permute-done.14 = f32[640,256]{1,0:T(8,128)S(1)} collective-permute-done((f32[640,256]{1,0:T(8,128)S(1)}, f32[640,256]{1,0:T(8,128)S(1)}, u32[]{:S(2)}, u32[]{:S(2)}) %collective-permute-start.14) | collective-permute-done | bytes 655392 | tf_op jit(solution)/shard_map/ppermute | solution.py:89
  138.9 16.9 %shard_map.73.a = f32[1024,2048]{1,0:T(8,128)S(1)} custom-call(s32[64]{0:T(128)S(1)} %dynamic-slice_bitcast_fusion.tab, f32[1024,2048]{1,0:T(8,128)} %a.1, f32[1024,256]{1,0:T(8,128)S(1)} %pad_maximum_fusion.2.p0, f32[1024,256]{1,0:T(8,128)S(1)} %pad_maximum_fusion.3.p1, f32[512,512]{1,0:T(8,128)S(1)} %pad_maximum_fusion.4.wk, ...), custom_call_target="tpu_custom_call" | custom-call | flops 11274289152 | bytes 27262976 | tf_op jit(solution)/shard_map/pallas_call | solution.py:354
  156.1 12.9 %shard_map.74 = (f32[1024,2048]{1,0:T(8,128)}, f32[512,1024]{1,0:T(8,128)}) custom-call(s32[64]{0:T(128)S(1)} %dynamic-slice_bitcast_fusion.tab, f32[1024,2048]{1,0:T(8,128)S(1)} %shard_map.73.a, f32[1024,256]{1,0:T(8,128)S(1)} %slice.279.p0, f32[1024,256]{1,0:T(8,128)S(1)} %slice.281.p1, bf16[1024,512]{1,0:T(8,128)(2,1)S(1)} %get-tuple-element.44.rh.xh, ...), custom_call_target="tpu_custom_call" | custom-call | flops 4831838208 | bytes 27262976 | tf_op jit(solution)/shard_map/pallas_call | solution.py:379
  (142 shorter events, 33.4 us)
Async XLA Ops:
  1.7 9.2 %collective-permute-start = (f32[128,256]{1,0:T(8,128)S(1)}, f32[128,256]{1,0:T(8,128)S(1)}, u32[]{:S(2)}, u32[]{:S(2)}) collective-permute-start(f32[128,256]{1,0:T(8,128)S(1)} %get-tuple-element.25), channel_id=1, source_target_pairs={{0,32},{1,33},{2,10},{3,11},{4,36},{5,37},{6,14},{7,15},{8,40},{9,... | collective-permute-start | bytes 393224 | tf_op jit(solution)/shard_map/ppermute | solution.py:89
  3.3 7.5 %collective-permute-start.1 = (f32[128,256]{1,0:T(8,128)S(1)}, f32[128,256]{1,0:T(8,128)S(1)}, u32[]{:S(2)}, u32[]{:S(2)}) collective-permute-start(f32[128,256]{1,0:T(8,128)S(1)} %get-tuple-element.27), channel_id=1, source_target_pairs={{0,96},{1,97},{2,26},{3,27},{4,100},{5,101},{6,30},{7,31},{8,104},... | collective-permute-start | bytes 393224 | tf_op jit(solution)/shard_map/ppermute | solution.py:89
  10.9 9.3 %collective-permute-start.2 = (f32[512,256]{1,0:T(8,128)S(1)}, f32[512,256]{1,0:T(8,128)S(1)}, u32[]{:S(2)}, u32[]{:S(2)}) collective-permute-start(f32[512,256]{1,0:T(8,128)S(1)} %pad_maximum_fusion.8), channel_id=1, source_target_pairs={{0,8},{1,9},{2,34},{3,35},{4,12},{5,13},{6,38},{7,39},{8,0},{9,1},... | collective-permute-start | bytes 1572872 | tf_op jit(solution)/shard_map/ppermute | solution.py:89
  12.9 10.4 %collective-permute-start.3 = (f32[512,256]{1,0:T(8,128)S(1)}, f32[512,256]{1,0:T(8,128)S(1)}, u32[]{:S(2)}, u32[]{:S(2)}) collective-permute-start(f32[512,256]{1,0:T(8,128)S(1)} %pad_maximum_fusion.9), channel_id=1, source_target_pairs={{0,24},{1,25},{2,98},{3,99},{4,28},{5,29},{6,102},{7,103},{8,16},{... | collective-permute-start | bytes 1572872 | tf_op jit(solution)/shard_map/ppermute | solution.py:89
  24.4 10.6 %collective-permute-start.5 = (f32[640,256]{1,0:T(8,128)S(1)}, f32[640,256]{1,0:T(8,128)S(1)}, u32[]{:S(2)}, u32[]{:S(2)}) collective-permute-start(f32[640,256]{1,0:T(8,128)S(1)} %pad_maximum_fusion.7), channel_id=1, source_target_pairs={{0,32},{1,33},{2,10},{3,11},{4,36},{5,37},{6,14},{7,15},{8,40},{9,... | collective-permute-start | bytes 1966088 | tf_op jit(solution)/shard_map/ppermute | solution.py:89
  25.0 11.8 %collective-permute-start.4 = (f32[640,256]{1,0:T(8,128)S(1)}, f32[640,256]{1,0:T(8,128)S(1)}, u32[]{:S(2)}, u32[]{:S(2)}) collective-permute-start(f32[640,256]{1,0:T(8,128)S(1)} %pad_maximum_fusion.6), channel_id=1, source_target_pairs={{0,96},{1,97},{2,26},{3,27},{4,100},{5,101},{6,30},{7,31},{8,104},... | collective-permute-start | bytes 1966088 | tf_op jit(solution)/shard_map/ppermute | solution.py:89
  36.9 16.8 %collective-permute-start.6 = (f32[1088,256]{1,0:T(8,128)S(1)}, f32[1088,256]{1,0:T(8,128)S(1)}, u32[]{:S(2)}, u32[]{:S(2)}) collective-permute-start(f32[1088,256]{1,0:T(8,128)S(1)} %constant_dynamic-update-slice_fusion), channel_id=1, source_target_pairs={{0,24},{1,25},{2,98},{3,99},{4,28},{5,29},{6,102},{7,103},{8,16},{... | collective-permute-start | bytes 3342344 | tf_op jit(solution)/shard_map/ppermute | solution.py:89
  39.5 15.7 %collective-permute-start.7 = (f32[1088,256]{1,0:T(8,128)}, f32[1088,256]{1,0:T(8,128)S(1)}, u32[]{:S(2)}, u32[]{:S(2)}) collective-permute-start(f32[1088,256]{1,0:T(8,128)} %copy-done.4), channel_id=1, source_target_pairs={{0,8},{1,9},{2,34},{3,35},{4,12},{5,13},{6,38},{7,39},{8,0},{9,1},... | collective-permute-start | bytes 3342344 | tf_op jit(solution)/shard_map/ppermute | solution.py:89
  66.8 12.1 %collective-permute-start.10 = (f32[384,512]{1,0:T(8,128)S(1)}, f32[384,512]{1,0:T(8,128)S(1)}, u32[]{:S(2)}, u32[]{:S(2)}) collective-permute-start(f32[384,512]{1,0:T(8,128)S(1)} %pad_maximum_fusion.5), channel_id=1, source_target_pairs={{0,4},{1,5},{2,7},{3,6},{4,0},{5,1},{6,3},{7,2},{8,12},{9,13},{10,... | collective-permute-start | bytes 2359304 | tf_op jit(solution)/shard_map/ppermute | solution.py:89
  79.2 9.1 %collective-permute-start.11 = (f32[192,512]{1,0:T(8,128)S(1)}, f32[192,512]{1,0:T(8,128)S(1)}, u32[]{:S(2)}, u32[]{:S(2)}) collective-permute-start(f32[192,512]{1,0:T(8,128)S(1)} %pad_maximum_fusion.12), channel_id=1, source_target_pairs={{0,5},{1,4},{2,6},{3,7},{4,1},{5,0},{6,2},{7,3},{8,13},{9,12},{10,... | collective-permute-start | bytes 1179656 | tf_op jit(solution)/shard_map/ppermute | solution.py:89
  90.4 7.2 %collective-permute-start.15 = (f32[192,256]{1,0:T(8,128)S(1)}, f32[192,256]{1,0:T(8,128)S(1)}, u32[]{:S(2)}, u32[]{:S(2)}) collective-permute-start(f32[192,256]{1,0:T(8,128)S(1)} %pad_maximum_fusion.19), channel_id=1, source_target_pairs={{0,96},{1,97},{2,26},{3,27},{4,100},{5,101},{6,30},{7,31},{8,104},... | collective-permute-start | bytes 589832 | tf_op jit(solution)/shard_map/ppermute | solution.py:89
  90.6 16.9 %collective-permute-start.18 = (f32[128,512]{1,0:T(8,128)S(1)}, f32[128,512]{1,0:T(8,128)S(1)}, u32[]{:S(2)}, u32[]{:S(2)}) collective-permute-start(f32[128,512]{1,0:T(8,128)S(1)} %slice_add_fusion), channel_id=1, source_target_pairs={{0,4},{1,5},{2,7},{3,6},{4,0},{5,1},{6,3},{7,2},{8,12},{9,13},{10,... | collective-permute-start | bytes 786440 | tf_op jit(solution)/shard_map/ppermute | solution.py:89
  91.1 7.3 %collective-permute-start.12 = (f32[192,256]{1,0:T(8,128)S(1)}, f32[192,256]{1,0:T(8,128)S(1)}, u32[]{:S(2)}, u32[]{:S(2)}) collective-permute-start(f32[192,256]{1,0:T(8,128)S(1)} %pad_maximum_fusion.18), channel_id=1, source_target_pairs={{0,32},{1,33},{2,10},{3,11},{4,36},{5,37},{6,14},{7,15},{8,40},{9,... | collective-permute-start | bytes 589832 | tf_op jit(solution)/shard_map/ppermute | solution.py:89
  97.6 14.2 %collective-permute-start.16 = (f32[320,256]{1,0:T(8,128)S(1)}, f32[320,256]{1,0:T(8,128)S(1)}, u32[]{:S(2)}, u32[]{:S(2)}) collective-permute-start(f32[320,256]{1,0:T(8,128)S(1)} %pad_maximum_fusion.14), channel_id=1, source_target_pairs={{0,24},{1,25},{2,98},{3,99},{4,28},{5,29},{6,102},{7,103},{8,16},{... | collective-permute-start | bytes 983048 | tf_op jit(solution)/shard_map/ppermute | solution.py:89
  104.7 7.0 %collective-permute-start.24 = (f32[64,512]{1,0:T(8,128)S(1)}, f32[64,512]{1,0:T(8,128)S(1)}, u32[]{:S(2)}, u32[]{:S(2)}) collective-permute-start(f32[64,512]{1,0:T(8,128)S(1)} %add.104), channel_id=1, source_target_pairs={{0,24},{1,25},{2,98},{3,99},{4,28},{5,29},{6,102},{7,103},{8,16},{... | collective-permute-start | bytes 393224 | tf_op jit(solution)/shard_map/ppermute | solution.py:89
  107.4 9.5 %collective-permute-start.13 = (f32[320,256]{1,0:T(8,128)S(1)}, f32[320,256]{1,0:T(8,128)S(1)}, u32[]{:S(2)}, u32[]{:S(2)}) collective-permute-start(f32[320,256]{1,0:T(8,128)S(1)} %pad_maximum_fusion.13), channel_id=1, source_target_pairs={{0,8},{1,9},{2,34},{3,35},{4,12},{5,13},{6,38},{7,39},{8,0},{9,1},... | collective-permute-start | bytes 983048 | tf_op jit(solution)/shard_map/ppermute | solution.py:89
  107.6 15.3 %collective-permute-start.19 = (f32[256,512]{1,0:T(8,128)S(1)}, f32[256,512]{1,0:T(8,128)S(1)}, u32[]{:S(2)}, u32[]{:S(2)}) collective-permute-start(f32[256,512]{1,0:T(8,128)S(1)} %pad_maximum_fusion.10), channel_id=1, source_target_pairs={{0,5},{1,4},{2,6},{3,7},{4,1},{5,0},{6,2},{7,3},{8,13},{9,12},{10,... | collective-permute-start | bytes 1572872 | tf_op jit(solution)/shard_map/ppermute | solution.py:89
  111.9 14.9 %collective-permute-start.17 = (f32[640,256]{1,0:T(8,128)S(1)}, f32[640,256]{1,0:T(8,128)S(1)}, u32[]{:S(2)}, u32[]{:S(2)}) collective-permute-start(f32[640,256]{1,0:T(8,128)S(1)} %get-tuple-element.73), channel_id=1, source_target_pairs={{0,32},{1,33},{2,10},{3,11},{4,36},{5,37},{6,14},{7,15},{8,40},{9,... | collective-permute-start | bytes 1966088 | tf_op jit(solution)/shard_map/ppermute | solution.py:89
  118.2 8.5 %collective-permute-start.26 = (f32[128,512]{1,0:T(8,128)S(1)}, f32[128,512]{1,0:T(8,128)S(1)}, u32[]{:S(2)}, u32[]{:S(2)}) collective-permute-start(f32[128,512]{1,0:T(8,128)S(1)} %pad_maximum_fusion.15), channel_id=1, source_target_pairs={{0,5},{1,4},{2,6},{3,7},{4,1},{5,0},{6,2},{7,3},{8,13},{9,12},{10,... | collective-permute-start | bytes 786440 | tf_op jit(solution)/shard_map/ppermute | solution.py:89
  122.4 14.2 %collective-permute-start.14 = (f32[640,256]{1,0:T(8,128)S(1)}, f32[640,256]{1,0:T(8,128)S(1)}, u32[]{:S(2)}, u32[]{:S(2)}) collective-permute-start(f32[640,256]{1,0:T(8,128)S(1)} %get-tuple-element.75), channel_id=1, source_target_pairs={{0,96},{1,97},{2,26},{3,27},{4,100},{5,101},{6,30},{7,31},{8,104},... | collective-permute-start | bytes 1966088 | tf_op jit(solution)/shard_map/ppermute | solution.py:89
  123.0 15.9 %collective-permute-start.20 = (f32[512,512]{1,0:T(8,128)S(1)}, f32[512,512]{1,0:T(8,128)S(1)}, u32[]{:S(2)}, u32[]{:S(2)}) collective-permute-start(f32[512,512]{1,0:T(8,128)S(1)} %pad_maximum_fusion.4.wk), channel_id=1, source_target_pairs={{0,2},{1,3},{2,0},{3,1},{4,6},{5,7},{6,4},{7,5},{8,10},{9,11},{10,... | collective-permute-start | bytes 3145736 | tf_op jit(solution)/shard_map/ppermute | solution.py:89
  126.8 12.1 %collective-permute-start.27 = (f32[256,512]{1,0:T(8,128)S(1)}, f32[256,512]{1,0:T(8,128)S(1)}, u32[]{:S(2)}, u32[]{:S(2)}) collective-permute-start(f32[256,512]{1,0:T(8,128)S(1)} %pad_maximum_fusion.11.gk), channel_id=1, source_target_pairs={{0,2},{1,3},{2,0},{3,1},{4,6},{5,7},{6,4},{7,5},{8,10},{9,11},{10,... | collective-permute-start | bytes 1572872 | tf_op jit(solution)/shard_map/ppermute | solution.py:89
  127.0 28.8 %collective-permute-start.29 = (f32[1280,256]{1,0:T(8,128)S(1)}, f32[1280,256]{1,0:T(8,128)S(1)}, u32[]{:S(2)}, u32[]{:S(2)}) collective-permute-start(f32[1280,256]{1,0:T(8,128)S(1)} %get-tuple-element.55), channel_id=1, source_target_pairs={{0,8},{1,9},{2,34},{3,35},{4,12},{5,13},{6,38},{7,39},{8,0},{9,1},... | collective-permute-start | bytes 3932168 | tf_op jit(solution)/shard_map/ppermute | solution.py:89
  136.8 19.2 %collective-permute-start.28 = (f32[1280,256]{1,0:T(8,128)S(1)}, f32[1280,256]{1,0:T(8,128)S(1)}, u32[]{:S(2)}, u32[]{:S(2)}) collective-permute-start(f32[1280,256]{1,0:T(8,128)S(1)} %get-tuple-element.57), channel_id=1, source_target_pairs={{0,24},{1,25},{2,98},{3,99},{4,28},{5,29},{6,102},{7,103},{8,16},{... | collective-permute-start | bytes 3932168 | tf_op jit(solution)/shard_map/ppermute | solution.py:89
  (15 other events, 90.2 us)

commit v3 on v2

--- a/solution.py
+++ b/solution.py
@@ -317,7 +317,8 @@
         place_cat((p0, p1), b3)
         for base, gsrc, wsrc in ((36, gk, wk), (32, gs, ws)):
             for i in range(4):
-                at = pl.ds(pl.multiple_of(tab[base + i] * 64, 64), 64)
+                at = tab[base + (0, 2, 1, 3)[i]] * 64
+                at = pl.ds(pl.multiple_of(at, 64), 64)
                 g[at, :] = gsrc[i * 64 : i * 64 + 64, :]
                 at = pl.ds(pl.multiple_of(tab[base + i] * 128, 128), 128)
                 w[at, :] = wsrc[i * 128 : i * 128 + 128, :]
@@ -435,30 +436,28 @@
     g = g_keep + moved(g_send, lambda c: "c")
     w, g = w.reshape(4, 128, 512), g.reshape(4, 64, 512)
     ch, cl, rh, rl = turned(tab, tfactor, reflectors, (v[0], last_v[0], v[1], last_v[1]))
-    for s in range(2):
-        w = w.reshape(-1, 2, 128, 512)
-        g = g.reshape(-1, 2, 64, 512)
-        n = w.shape[0]
-        message = jnp.concatenate(
-            [w[:, 1].reshape(n * 128, 512), g[:, 1].reshape(n * 64, 512)], axis=0
-        )
-        if s == 1:
-            message, ch, cl, rh, rl = lax.optimization_barrier((message, ch, cl, rh, rl))
-        got = moved(message, lambda c: y_dim(c, s))
-        w = w[:, 0] + got[: n * 128].reshape(n, 128, 512)
-        g = g[:, 0] + got[n * 128 :].reshape(n, 64, 512)
-    w, g = w.reshape(128, 512), g.reshape(64, 512)
+    message = jnp.concatenate(
+        [w[1::2].reshape(256, 512), g[1::2].reshape(128, 512)], axis=0
+    )
+    got = moved(message, lambda c: y_dim(c, 0))
+    w = w[::2].reshape(256, 512) + got[:256]
+    g = g[::2].reshape(128, 512) + got[256:]
+    w, g, ch, cl, rh, rl = lax.optimization_barrier((w, g, ch, cl, rh, rl))
+    w = w[:128] + moved(w[128:], lambda c: y_dim(c, 1))
+    g = g + moved(g, lambda c: row_dim(c, 0, 3))
 
     wc = [w[:, :256], w[:, 256:]]
     last_w, last_q = [None, None], [None, None]
     w_rows = w
     for s in range(4):
-        g = g + moved(g, lambda c: row_dim(c, 0, s))
-        for h in range(2):
+        messages = [jnp.concatenate([wc[h], q[h]], axis=0) for h in range(2)]
+        if s < 2:
+            m0, m1, g, w_rows = lax.optimization_barrier((*messages, g, w_rows))
+        else:
+            m0, m1 = lax.optimization_barrier(messages)
+        for h, message in enumerate((m0, m1)):
             n = wc[h].shape[0]
-            got = moved(
-                jnp.concatenate([wc[h], q[h]], axis=0), lambda c: row_dim(c, h, s)
-            )
+            got = moved(message, lambda c: row_dim(c, h, s))
             if s == 0:
                 q[h] = q[h] + jnp.concatenate([got[n + 32 :], got[n : n + 32]], axis=0)
             elif s < 3:
@@ -469,13 +468,16 @@
                 wc[h] = jnp.concatenate([wc[h], got[:n]], axis=0)
             else:
                 last_w[h] = got[:n]
+        if s < 3:
+            g = g + moved(g, lambda c: row_dim(c, 0, s))
         if s < 2:
             w_rows = jnp.concatenate(
                 [w_rows, moved(w_rows, lambda c: y_dim(c, s))], axis=0
             )
     w_other = moved(w_rows, lambda c: "c")
-    for s in range(2):
-        g = jnp.concatenate([g, moved(g, lambda c: y_dim(c, s))], axis=0)
+    got = moved(g, lambda c: y_dim(c, 1))
+    g = g + jnp.concatenate([got[64:], got[:64]], axis=0)
+    g = jnp.concatenate([g, moved(g, lambda c: y_dim(c, 0))], axis=0)
     g_other = moved(g, lambda c: "c")
 
     part = update_first(tab, matrix, wc, w_rows, w_other, g, g_other, rh, rl, ch, cl)

time: 169 us -> 166 us (0.982); the launches traced: 169 us -> 164 us
  starting transfers between devices: 38.5 us -> 33.4 us
    ppermute x30, starting transfers between devices: 38.5 us -> 33.4 us  [moved(): return lax.ppermute(x, EVERY, pairs)]
  transfers between devices with their start and end apart: 30 -> 30, of which waited for: 16 -> 21; matrix products, arithmetic and copies ran while one was open for 2% -> 2% of each run, Pallas kernels for 21% -> 22%
where the time goes in v3:
time: 166 us; the launch traced here: 164 us
  waiting for transfers between devices  67.6 us (41%)
  Pallas kernels  55.2 us (33%)
  starting transfers between devices  33.4 us (20%)
  local copies, waits for them, and re-layouts  3.86 us (2%)
  other arithmetic  2.38 us (1%)
    ppermute x30, waiting for transfers between devices, moved(): return lax.ppermute(x, EVERY, pairs)  67.6 us
    ppermute x30, starting transfers between devices, moved(): return lax.ppermute(x, EVERY, pairs)  33.4 us
    pallas_call x1, Pallas kernels, update_first(): pl.pallas_call(update_first_kernel, grid_spec=pltpu.PrefetchScalarGridSpe...  17 us
    pallas_call x1, Pallas kernels, update_last(): pl.pallas_call(update_last_kernel, grid_spec=pltpu.PrefetchScalarGridSpec...  12.9 us
    pallas_call x2, Pallas kernels, apply_matrix(): pl.pallas_call(apply_last_kernel if last else apply_first_kernel, grid_sp...  11.9 us
    pallas_call x1, Pallas kernels, turned(): pl.pallas_call(turned_kernel, grid_spec=pltpu.PrefetchScalarGridSpec(num_...  6.34 us
    pallas_call x1, Pallas kernels, basis_product(): pl.pallas_call(basis_kernel, grid_spec=pltpu.PrefetchScalarGridSpec(num_s...  4.62 us
  transfers between devices with their start and end apart: 30, of which 21 were waited for; matrix products, arithmetic and copies ran while one was open for 2% of the time, Pallas kernels for 22%

profile of v3, /device:TPU:0, one launch (start us, length us, event | category | flops | bytes accessed | tf_op | source)
XLA Modules:
  0.0 163.8 jit_solution(12671705617994301791)
XLA Ops:
  6.1 4.6 %shard_map.68 = (f32[512,256]{1,0:T(8,128)S(1)}, f32[512,256]{1,0:T(8,128)S(1)}) custom-call(s32[64]{0:T(128)S(1)} %dynamic-slice_bitcast_fusion.tab, f32[512,1024]{1,0:T(8,128)} %b_ref.3, f32[1024,512]{1,0:T(8,128)} %v_ref.5), custom_call_target="tpu_custom_call" | custom-call | flops 1610612736 | bytes 5242880 | tf_op jit(solution)/shard_map/pallas_call | solution.py:141
  15.4 4.7 %collective-permute-done.2 = f32[512,256]{1,0:T(8,128)S(1)} collective-permute-done((f32[512,256]{1,0:T(8,128)S(1)}, f32[512,256]{1,0:T(8,128)S(1)}, u32[]{:S(2)}, u32[]{:S(2)}) %collective-permute-start.2) | collective-permute-done | bytes 524320 | tf_op jit(solution)/shard_map/ppermute | solution.py:89
  20.1 3.1 %collective-permute-done.3 = f32[512,256]{1,0:T(8,128)S(1)} collective-permute-done((f32[512,256]{1,0:T(8,128)S(1)}, f32[512,256]{1,0:T(8,128)S(1)}, u32[]{:S(2)}, u32[]{:S(2)}) %collective-permute-start.3) | collective-permute-done | bytes 524320 | tf_op jit(solution)/shard_map/ppermute | solution.py:89
  25.6 9.4 %collective-permute-done.5 = f32[640,256]{1,0:T(8,128)S(1)} collective-permute-done((f32[640,256]{1,0:T(8,128)S(1)}, f32[640,256]{1,0:T(8,128)S(1)}, u32[]{:S(2)}, u32[]{:S(2)}) %collective-permute-start.5) | collective-permute-done | bytes 655392 | tf_op jit(solution)/shard_map/ppermute | solution.py:89
  36.9 2.6 %collective-permute-start.6 = (f32[1088,256]{1,0:T(8,128)S(1)}, f32[1088,256]{1,0:T(8,128)S(1)}, u32[]{:S(2)}, u32[]{:S(2)}) collective-permute-start(f32[1088,256]{1,0:T(8,128)S(1)} %constant_dynamic-update-slice_fusion), channel_id=1, source_target_pairs={{0,24},{1,25},{2,98},{3,99},{4,28},{5,29},{6,102},{7,103},{8,16},{... | collective-permute-start | bytes 3342344 | tf_op jit(solution)/shard_map/ppermute | solution.py:89
  39.8 5.8 %shard_map.69.acc = f32[1024,512]{1,0:T(8,128)S(1)} custom-call(s32[64]{0:T(128)S(1)} %dynamic-slice_bitcast_fusion.tab, f32[1024,2048]{1,0:T(8,128)S(1)} %bitcast.11, f32[1024,2048]{1,0:T(8,128)S(1)} %bitcast.11, f32[1024,2048]{1,0:T(8,128)S(1)} %bitcast.11, f32[1024,2048]{1,0:T(8,128)S(1)} %bitcast.11, f32[1024,256]{1,0:T(8,128)S(1)} %pad_maximum_fusion.p0, ...), custom_call_target="tpu_custom_call" | custom-call | flops 3221225472 | bytes 12582912 | tf_op jit(solution)/shard_map/pallas_call | solution.py:203
  45.7 8.1 %collective-permute-done.6 = f32[1088,256]{1,0:T(8,128)S(1)} collective-permute-done((f32[1088,256]{1,0:T(8,128)S(1)}, f32[1088,256]{1,0:T(8,128)S(1)}, u32[]{:S(2)}, u32[]{:S(2)}) %collective-permute-start.6) | collective-permute-done | bytes 1114144 | tf_op jit(solution)/shard_map/ppermute | solution.py:89
  55.3 6.1 %shard_map.70 = (f32[512,512]{1,0:T(8,128)S(1)}, f32[512,512]{1,0:T(8,128)S(1)}) custom-call(s32[64]{0:T(128)S(1)} %dynamic-slice_bitcast_fusion.tab, f32[1024,2048]{1,0:T(8,128)S(1)} %bitcast.11, f32[1024,2048]{1,0:T(8,128)S(1)} %bitcast.11, f32[1024,2048]{1,0:T(8,128)S(1)} %bitcast.11, f32[1024,2048]{1,0:T(8,128)S(1)} %bitcast.11, ...), custom_call_target="tpu_custom_call" | custom-call | flops 3221225472 | bytes 12582912 | tf_op jit(solution)/shard_map/pallas_call | solution.py:203
  68.6 6.3 %shard_map.72 = (bf16[2048,512]{1,0:T(8,128)(2,1)S(1)}, bf16[2048,512]{1,0:T(8,128)(2,1)S(1)}, bf16[1024,512]{1,0:T(8,128)(2,1)S(1)}, bf16[1024,512]{1,0:T(8,128)(2,1)S(1)}) custom-call(s32[64]{0:T(128)S(1)} %dynamic-slice_bitcast_fusion.tab, f32[512,512]{1,0:T(8,128)S(1)} %copy-done.2, f32[1024,512]{1,0:T(8,128)S(1)} %copy-done.1, ...), custom_call_target="tpu_custom_call" | custom-call | flops 4831838208 | bytes 13631488 | tf_op jit(solution)/shard_map/pallas_call | solution.py:268
  74.9 4.0 %collective-permute-done.10 = f32[384,512]{1,0:T(8,128)S(1)} collective-permute-done((f32[384,512]{1,0:T(8,128)S(1)}, f32[384,512]{1,0:T(8,128)S(1)}, u32[]{:S(2)}, u32[]{:S(2)}) %collective-permute-start.10) | collective-permute-done | bytes 786464 | tf_op jit(solution)/shard_map/ppermute | solution.py:89
  79.1 3.1 %collective-permute-start.11 = (f32[128,512]{1,0:T(8,128)S(1)}, f32[128,512]{1,0:T(8,128)S(1)}, u32[]{:S(2)}, u32[]{:S(2)}) collective-permute-start(f32[128,512]{1,0:T(8,128)S(1)} %slice.197), channel_id=1, source_target_pairs={{0,5},{1,4},{2,6},{3,7},{4,1},{5,0},{6,2},{7,3},{8,13},{9,12},{10,... | collective-permute-start | bytes 786440 | tf_op jit(solution)/shard_map/ppermute | solution.py:89
  84.0 2.7 %collective-permute-done.11 = f32[128,512]{1,0:T(8,128)S(1)} collective-permute-done((f32[128,512]{1,0:T(8,128)S(1)}, f32[128,512]{1,0:T(8,128)S(1)}, u32[]{:S(2)}, u32[]{:S(2)}) %collective-permute-start.11) | collective-permute-done | bytes 262176 | tf_op jit(solution)/shard_map/ppermute | solution.py:89
  86.9 3.8 %collective-permute-done.12 = f32[128,512]{1,0:T(8,128)S(1)} collective-permute-done((f32[128,512]{1,0:T(8,128)S(1)}, f32[128,512]{1,0:T(8,128)S(1)}, u32[]{:S(2)}, u32[]{:S(2)}) %collective-permute-start.12) | collective-permute-done | bytes 262176 | tf_op jit(solution)/shard_map/ppermute | solution.py:89
  93.1 3.5 %collective-permute-done.13 = f32[192,256]{1,0:T(8,128)S(1)} collective-permute-done((f32[192,256]{1,0:T(8,128)S(1)}, f32[192,256]{1,0:T(8,128)S(1)}, u32[]{:S(2)}, u32[]{:S(2)}) %collective-permute-start.13) | collective-permute-done | bytes 196640 | tf_op jit(solution)/shard_map/ppermute | solution.py:89
  96.6 3.6 %collective-permute-done.14 = f32[192,256]{1,0:T(8,128)S(1)} collective-permute-done((f32[192,256]{1,0:T(8,128)S(1)}, f32[192,256]{1,0:T(8,128)S(1)}, u32[]{:S(2)}, u32[]{:S(2)}) %collective-permute-start.14) | collective-permute-done | bytes 196640 | tf_op jit(solution)/shard_map/ppermute | solution.py:89
  103.4 4.3 %collective-permute-done.23 = f32[128,512]{1,0:T(8,128)S(1)} collective-permute-done((f32[128,512]{1,0:T(8,128)S(1)}, f32[128,512]{1,0:T(8,128)S(1)}, u32[]{:S(2)}, u32[]{:S(2)}) %collective-permute-start.23) | collective-permute-done | bytes 262176 | tf_op jit(solution)/shard_map/ppermute | solution.py:89
  107.7 3.0 %collective-permute-start.24 = (f32[128,512]{1,0:T(8,128)S(1)}, f32[128,512]{1,0:T(8,128)S(1)}, u32[]{:S(2)}, u32[]{:S(2)}) collective-permute-start(f32[128,512]{1,0:T(8,128)S(1)} %add.87), channel_id=1, source_target_pairs={{0,96},{1,97},{2,26},{3,27},{4,100},{5,101},{6,30},{7,31},{8,104},... | collective-permute-start | bytes 786440 | tf_op jit(solution)/shard_map/ppermute | solution.py:89
  112.4 3.0 %collective-permute-done.24 = f32[128,512]{1,0:T(8,128)S(1)} collective-permute-done((f32[128,512]{1,0:T(8,128)S(1)}, f32[128,512]{1,0:T(8,128)S(1)}, u32[]{:S(2)}, u32[]{:S(2)}) %collective-permute-start.24) | collective-permute-done | bytes 262176 | tf_op jit(solution)/shard_map/ppermute | solution.py:89
  115.6 3.0 %collective-permute-start.19 = (f32[640,256]{1,0:T(8,128)S(1)}, f32[640,256]{1,0:T(8,128)S(1)}, u32[]{:S(2)}, u32[]{:S(2)}) collective-permute-start(f32[640,256]{1,0:T(8,128)S(1)} %get-tuple-element.64), channel_id=1, source_target_pairs={{0,96},{1,97},{2,26},{3,27},{4,100},{5,101},{6,30},{7,31},{8,104},... | collective-permute-start | bytes 1966088 | tf_op jit(solution)/shard_map/ppermute | solution.py:89
  119.1 4.0 %collective-permute-done.25 = f32[128,512]{1,0:T(8,128)S(1)} collective-permute-done((f32[128,512]{1,0:T(8,128)S(1)}, f32[128,512]{1,0:T(8,128)S(1)}, u32[]{:S(2)}, u32[]{:S(2)}) %collective-permute-start.25) | collective-permute-done | bytes 262176 | tf_op jit(solution)/shard_map/ppermute | solution.py:89
  123.3 4.2 %collective-permute-done.19 = f32[640,256]{1,0:T(8,128)S(1)} collective-permute-done((f32[640,256]{1,0:T(8,128)S(1)}, f32[640,256]{1,0:T(8,128)S(1)}, u32[]{:S(2)}, u32[]{:S(2)}) %collective-permute-start.19) | collective-permute-done | bytes 655392 | tf_op jit(solution)/shard_map/ppermute | solution.py:89
  130.0 3.2 %collective-permute-start.28 = (f32[1280,256]{1,0:T(8,128)S(1)}, f32[1280,256]{1,0:T(8,128)S(1)}, u32[]{:S(2)}, u32[]{:S(2)}) collective-permute-start(f32[1280,256]{1,0:T(8,128)S(1)} %get-tuple-element.72), channel_id=1, source_target_pairs={{0,24},{1,25},{2,98},{3,99},{4,28},{5,29},{6,102},{7,103},{8,16},{... | collective-permute-start | bytes 3932168 | tf_op jit(solution)/shard_map/ppermute | solution.py:89
  133.5 17.0 %shard_map.73.a = f32[1024,2048]{1,0:T(8,128)S(1)} custom-call(s32[64]{0:T(128)S(1)} %dynamic-slice_bitcast_fusion.tab, f32[1024,2048]{1,0:T(8,128)} %a.1, f32[1024,256]{1,0:T(8,128)S(1)} %pad_maximum_fusion.2.p0, f32[1024,256]{1,0:T(8,128)S(1)} %pad_maximum_fusion.3.p1, f32[512,512]{1,0:T(8,128)S(1)} %constant_dynamic-update-slice_fusion.20.wk, ...), custom_call_target="tpu_custom_call" | custom-call | flops 11274289152 | bytes 27262976 | tf_op jit(solution)/shard_map/pallas_call | solution.py:355
  150.9 12.9 %shard_map.74 = (f32[1024,2048]{1,0:T(8,128)}, f32[512,1024]{1,0:T(8,128)}) custom-call(s32[64]{0:T(128)S(1)} %dynamic-slice_bitcast_fusion.tab, f32[1024,2048]{1,0:T(8,128)S(1)} %shard_map.73.a, f32[1024,256]{1,0:T(8,128)S(1)} %slice.264.p0, f32[1024,256]{1,0:T(8,128)S(1)} %slice.265.p1, bf16[1024,512]{1,0:T(8,128)(2,1)S(1)} %get-tuple-element.68.rh.xh, ...), custom_call_target="tpu_custom_call" | custom-call | flops 4831838208 | bytes 27262976 | tf_op jit(solution)/shard_map/pallas_call | solution.py:380
  (139 shorter events, 36.5 us)
Async XLA Ops:
  1.7 9.2 %collective-permute-start = (f32[128,256]{1,0:T(8,128)S(1)}, f32[128,256]{1,0:T(8,128)S(1)}, u32[]{:S(2)}, u32[]{:S(2)}) collective-permute-start(f32[128,256]{1,0:T(8,128)S(1)} %get-tuple-element.38), channel_id=1, source_target_pairs={{0,32},{1,33},{2,10},{3,11},{4,36},{5,37},{6,14},{7,15},{8,40},{9,... | collective-permute-start | bytes 393224 | tf_op jit(solution)/shard_map/ppermute | solution.py:89
  3.3 7.5 %collective-permute-start.1 = (f32[128,256]{1,0:T(8,128)S(1)}, f32[128,256]{1,0:T(8,128)S(1)}, u32[]{:S(2)}, u32[]{:S(2)}) collective-permute-start(f32[128,256]{1,0:T(8,128)S(1)} %get-tuple-element.40), channel_id=1, source_target_pairs={{0,96},{1,97},{2,26},{3,27},{4,100},{5,101},{6,30},{7,31},{8,104},... | collective-permute-start | bytes 393224 | tf_op jit(solution)/shard_map/ppermute | solution.py:89
  10.9 9.3 %collective-permute-start.2 = (f32[512,256]{1,0:T(8,128)S(1)}, f32[512,256]{1,0:T(8,128)S(1)}, u32[]{:S(2)}, u32[]{:S(2)}) collective-permute-start(f32[512,256]{1,0:T(8,128)S(1)} %pad_maximum_fusion.7), channel_id=1, source_target_pairs={{0,8},{1,9},{2,34},{3,35},{4,12},{5,13},{6,38},{7,39},{8,0},{9,1},... | collective-permute-start | bytes 1572872 | tf_op jit(solution)/shard_map/ppermute | solution.py:89
  12.9 10.4 %collective-permute-start.3 = (f32[512,256]{1,0:T(8,128)S(1)}, f32[512,256]{1,0:T(8,128)S(1)}, u32[]{:S(2)}, u32[]{:S(2)}) collective-permute-start(f32[512,256]{1,0:T(8,128)S(1)} %pad_maximum_fusion.8), channel_id=1, source_target_pairs={{0,24},{1,25},{2,98},{3,99},{4,28},{5,29},{6,102},{7,103},{8,16},{... | collective-permute-start | bytes 1572872 | tf_op jit(solution)/shard_map/ppermute | solution.py:89
  24.4 10.6 %collective-permute-start.5 = (f32[640,256]{1,0:T(8,128)S(1)}, f32[640,256]{1,0:T(8,128)S(1)}, u32[]{:S(2)}, u32[]{:S(2)}) collective-permute-start(f32[640,256]{1,0:T(8,128)S(1)} %pad_maximum_fusion.6), channel_id=1, source_target_pairs={{0,32},{1,33},{2,10},{3,11},{4,36},{5,37},{6,14},{7,15},{8,40},{9,... | collective-permute-start | bytes 1966088 | tf_op jit(solution)/shard_map/ppermute | solution.py:89
  25.0 11.8 %collective-permute-start.4 = (f32[640,256]{1,0:T(8,128)S(1)}, f32[640,256]{1,0:T(8,128)S(1)}, u32[]{:S(2)}, u32[]{:S(2)}) collective-permute-start(f32[640,256]{1,0:T(8,128)S(1)} %pad_maximum_fusion.5), channel_id=1, source_target_pairs={{0,96},{1,97},{2,26},{3,27},{4,100},{5,101},{6,30},{7,31},{8,104},... | collective-permute-start | bytes 1966088 | tf_op jit(solution)/shard_map/ppermute | solution.py:89
  36.9 16.8 %collective-permute-start.6 = (f32[1088,256]{1,0:T(8,128)S(1)}, f32[1088,256]{1,0:T(8,128)S(1)}, u32[]{:S(2)}, u32[]{:S(2)}) collective-permute-start(f32[1088,256]{1,0:T(8,128)S(1)} %constant_dynamic-update-slice_fusion), channel_id=1, source_target_pairs={{0,24},{1,25},{2,98},{3,99},{4,28},{5,29},{6,102},{7,103},{8,16},{... | collective-permute-start | bytes 3342344 | tf_op jit(solution)/shard_map/ppermute | solution.py:89
  39.5 15.7 %collective-permute-start.7 = (f32[1088,256]{1,0:T(8,128)}, f32[1088,256]{1,0:T(8,128)S(1)}, u32[]{:S(2)}, u32[]{:S(2)}) collective-permute-start(f32[1088,256]{1,0:T(8,128)} %copy-done.4), channel_id=1, source_target_pairs={{0,8},{1,9},{2,34},{3,35},{4,12},{5,13},{6,38},{7,39},{8,0},{9,1},... | collective-permute-start | bytes 3342344 | tf_op jit(solution)/shard_map/ppermute | solution.py:89
  66.9 12.1 %collective-permute-start.10 = (f32[384,512]{1,0:T(8,128)S(1)}, f32[384,512]{1,0:T(8,128)S(1)}, u32[]{:S(2)}, u32[]{:S(2)}) collective-permute-start(f32[384,512]{1,0:T(8,128)S(1)} %pad_maximum_fusion.4), channel_id=1, source_target_pairs={{0,4},{1,5},{2,7},{3,6},{4,0},{5,1},{6,3},{7,2},{8,12},{9,13},{10,... | collective-permute-start | bytes 2359304 | tf_op jit(solution)/shard_map/ppermute | solution.py:89
  79.1 7.7 %collective-permute-start.11 = (f32[128,512]{1,0:T(8,128)S(1)}, f32[128,512]{1,0:T(8,128)S(1)}, u32[]{:S(2)}, u32[]{:S(2)}) collective-permute-start(f32[128,512]{1,0:T(8,128)S(1)} %slice.197), channel_id=1, source_target_pairs={{0,5},{1,4},{2,6},{3,7},{4,1},{5,0},{6,2},{7,3},{8,13},{9,12},{10,... | collective-permute-start | bytes 786440 | tf_op jit(solution)/shard_map/ppermute | solution.py:89
  83.1 7.7 %collective-permute-start.12 = (f32[128,512]{1,0:T(8,128)S(1)}, f32[128,512]{1,0:T(8,128)S(1)}, u32[]{:S(2)}, u32[]{:S(2)}) collective-permute-start(f32[128,512]{1,0:T(8,128)S(1)} %slice_add_fusion.1), channel_id=1, source_target_pairs={{0,24},{1,25},{2,98},{3,99},{4,28},{5,29},{6,102},{7,103},{8,16},{... | collective-permute-start | bytes 786440 | tf_op jit(solution)/shard_map/ppermute | solution.py:89
  92.9 7.3 %collective-permute-start.14 = (f32[192,256]{1,0:T(8,128)S(1)}, f32[192,256]{1,0:T(8,128)S(1)}, u32[]{:S(2)}, u32[]{:S(2)}) collective-permute-start(f32[192,256]{1,0:T(8,128)S(1)} %pad_maximum_fusion.16), channel_id=1, source_target_pairs={{0,96},{1,97},{2,26},{3,27},{4,100},{5,101},{6,30},{7,31},{8,104},... | collective-permute-start | bytes 589832 | tf_op jit(solution)/shard_map/ppermute | solution.py:89
  92.9 8.1 %collective-permute-start.15 = (f32[128,512]{1,0:T(8,128)S(1)}, f32[128,512]{1,0:T(8,128)S(1)}, u32[]{:S(2)}, u32[]{:S(2)}) collective-permute-start(f32[128,512]{1,0:T(8,128)S(1)} %add.83), channel_id=1, source_target_pairs={{0,32},{1,33},{2,10},{3,11},{4,36},{5,37},{6,14},{7,15},{8,40},{9,... | collective-permute-start | bytes 786440 | tf_op jit(solution)/shard_map/ppermute | solution.py:89
  93.1 8.0 %collective-permute-start.16 = (f32[128,512]{1,0:T(8,128)S(1)}, f32[128,512]{1,0:T(8,128)S(1)}, u32[]{:S(2)}, u32[]{:S(2)}) collective-permute-start(f32[128,512]{1,0:T(8,128)S(1)} %slice_add_fusion.4), channel_id=1, source_target_pairs={{0,4},{1,5},{2,7},{3,6},{4,0},{5,1},{6,3},{7,2},{8,12},{9,13},{10,... | collective-permute-start | bytes 786440 | tf_op jit(solution)/shard_map/ppermute | solution.py:89
  101.2 11.1 %collective-permute-start.18 = (f32[320,256]{1,0:T(8,128)S(1)}, f32[320,256]{1,0:T(8,128)S(1)}, u32[]{:S(2)}, u32[]{:S(2)}) collective-permute-start(f32[320,256]{1,0:T(8,128)S(1)} %pad_maximum_fusion.12), channel_id=1, source_target_pairs={{0,24},{1,25},{2,98},{3,99},{4,28},{5,29},{6,102},{7,103},{8,16},{... | collective-permute-start | bytes 983048 | tf_op jit(solution)/shard_map/ppermute | solution.py:89
  101.3 11.0 %collective-permute-start.17 = (f32[320,256]{1,0:T(8,128)S(1)}, f32[320,256]{1,0:T(8,128)S(1)}, u32[]{:S(2)}, u32[]{:S(2)}) collective-permute-start(f32[320,256]{1,0:T(8,128)S(1)} %pad_maximum_fusion.11), channel_id=1, source_target_pairs={{0,8},{1,9},{2,34},{3,35},{4,12},{5,13},{6,38},{7,39},{8,0},{9,1},... | collective-permute-start | bytes 983048 | tf_op jit(solution)/shard_map/ppermute | solution.py:89
  103.4 15.6 %collective-permute-start.21 = (f32[256,512]{1,0:T(8,128)S(1)}, f32[256,512]{1,0:T(8,128)S(1)}, u32[]{:S(2)}, u32[]{:S(2)}) collective-permute-start(f32[256,512]{1,0:T(8,128)S(1)} %pad_maximum_fusion.9), channel_id=1, source_target_pairs={{0,5},{1,4},{2,6},{3,7},{4,1},{5,0},{6,2},{7,3},{8,13},{9,12},{10,... | collective-permute-start | bytes 1572872 | tf_op jit(solution)/shard_map/ppermute | solution.py:89
  107.7 7.7 %collective-permute-start.24 = (f32[128,512]{1,0:T(8,128)S(1)}, f32[128,512]{1,0:T(8,128)S(1)}, u32[]{:S(2)}, u32[]{:S(2)}) collective-permute-start(f32[128,512]{1,0:T(8,128)S(1)} %add.87), channel_id=1, source_target_pairs={{0,96},{1,97},{2,26},{3,27},{4,100},{5,101},{6,30},{7,31},{8,104},... | collective-permute-start | bytes 786440 | tf_op jit(solution)/shard_map/ppermute | solution.py:89
  115.4 7.7 %collective-permute-start.25 = (f32[128,512]{1,0:T(8,128)S(1)}, f32[128,512]{1,0:T(8,128)S(1)}, u32[]{:S(2)}, u32[]{:S(2)}) collective-permute-start(f32[128,512]{1,0:T(8,128)S(1)} %add.88), channel_id=1, source_target_pairs={{0,5},{1,4},{2,6},{3,7},{4,1},{5,0},{6,2},{7,3},{8,13},{9,12},{10,... | collective-permute-start | bytes 786440 | tf_op jit(solution)/shard_map/ppermute | solution.py:89
  115.6 11.9 %collective-permute-start.19 = (f32[640,256]{1,0:T(8,128)S(1)}, f32[640,256]{1,0:T(8,128)S(1)}, u32[]{:S(2)}, u32[]{:S(2)}) collective-permute-start(f32[640,256]{1,0:T(8,128)S(1)} %get-tuple-element.64), channel_id=1, source_target_pairs={{0,96},{1,97},{2,26},{3,27},{4,100},{5,101},{6,30},{7,31},{8,104},... | collective-permute-start | bytes 1966088 | tf_op jit(solution)/shard_map/ppermute | solution.py:89
  118.6 10.7 %collective-permute-start.20 = (f32[640,256]{1,0:T(8,128)S(1)}, f32[640,256]{1,0:T(8,128)S(1)}, u32[]{:S(2)}, u32[]{:S(2)}) collective-permute-start(f32[640,256]{1,0:T(8,128)S(1)} %get-tuple-element.65), channel_id=1, source_target_pairs={{0,32},{1,33},{2,10},{3,11},{4,36},{5,37},{6,14},{7,15},{8,40},{9,... | collective-permute-start | bytes 1966088 | tf_op jit(solution)/shard_map/ppermute | solution.py:89
  119.0 14.4 %collective-permute-start.22 = (f32[512,512]{1,0:T(8,128)S(1)}, f32[512,512]{1,0:T(8,128)S(1)}, u32[]{:S(2)}, u32[]{:S(2)}) collective-permute-start(f32[512,512]{1,0:T(8,128)S(1)} %constant_dynamic-update-slice_fusion.20.wk), channel_id=1, source_target_pairs={{0,2},{1,3},{2,0},{3,1},{4,6},{5,7},{6,4},{7,5},{8,10},{9,11},{10,... | collective-permute-start | bytes 3145736 | tf_op jit(solution)/shard_map/ppermute | solution.py:89
  130.0 20.4 %collective-permute-start.28 = (f32[1280,256]{1,0:T(8,128)S(1)}, f32[1280,256]{1,0:T(8,128)S(1)}, u32[]{:S(2)}, u32[]{:S(2)}) collective-permute-start(f32[1280,256]{1,0:T(8,128)S(1)} %get-tuple-element.72), channel_id=1, source_target_pairs={{0,24},{1,25},{2,98},{3,99},{4,28},{5,29},{6,102},{7,103},{8,16},{... | collective-permute-start | bytes 3932168 | tf_op jit(solution)/shard_map/ppermute | solution.py:89
  133.2 17.6 %collective-permute-start.29 = (f32[1280,256]{1,0:T(8,128)S(1)}, f32[1280,256]{1,0:T(8,128)S(1)}, u32[]{:S(2)}, u32[]{:S(2)}) collective-permute-start(f32[1280,256]{1,0:T(8,128)S(1)} %get-tuple-element.73), channel_id=1, source_target_pairs={{0,8},{1,9},{2,34},{3,35},{4,12},{5,13},{6,38},{7,39},{8,0},{9,1},... | collective-permute-start | bytes 3932168 | tf_op jit(solution)/shard_map/ppermute | solution.py:89
  (15 other events, 89.7 us)
